TPU v7x, 32 devices: a whole 2x2x4 slice. The times are simulated.
32 devices in a mesh: dp: 8 (over z, x), head: 4 (over y, core).
Axes of the slice: x: 2, y: 2, z: 4, core: 2. Of those that a mesh axis runs over, the one named last changes fastest.
Arguments:
- queries: bfloat16 [4096, 2048], P('dp', 'head'), may hold values from -48 to 48
- encodings: bfloat16 [128, 128, 896], P('dp', None, 'head'), may hold values from -12 to 12
- neighbour_ids: int32 [64, 2], P('dp'), may hold values from 0 to 127, as said below
- block_place: int32 [128], replicated, may hold values from 0 to 127, as said below
- query_weight: bfloat16 [4096, 2048], P(None, 'head'), may hold values from -1 to 1
- key_weight: bfloat16 [896, 2048], P(None, 'head'), may hold values from -1 to 1
- value_weight: bfloat16 [896, 2048], P(None, 'head'), may hold values from -0.1875 to 0.1875
- attn_grad: bfloat16 [4096, 2048], P('dp', 'head'), may hold values from -24 to 24
Outputs:
- query_input_grad: bfloat16 [4096, 4096], P('dp', 'head')
- encodings_grad: bfloat16 [128, 128, 896], P('dp', None, 'head')
- key_weight_grad: float32 [896, 2048], P('dp', 'head')
- value_weight_grad: float32 [896, 2048], P('dp', 'head')
Inputs may be any that keep to these rules, and one draw needn't show every extreme that they name: `neighbour_ids`: block b is stored at position block_place[b] of encodings, on the index block_place[b] // 16 of dp. Of the 16 slots of the spans of one index of dp, each index of dp stores the blocks of 2 or 1, and some index stores those of exactly 2. `block_place`: A permutation: every position once.
All inputs are finite; a program needn't handle non-finite values.
Results may differ from a plain program's by a relative error of at most 0.012.
The roundings to bfloat16 on the way count: a program that leaves them out, or rounds other values in their place, can miss the bound.
Values may be sent and summed in bfloat16 or wider, within the bound.
A program may use at most 128 MiB of HBM per device.

v0:
```python
import math

import jax
import jax.numpy as jnp
from jax import lax
from jax.sharding import PartitionSpec as P

DH = 128
E = 896
CH = 64
NTOK = 128
NEIGH = 2


def shards(
    queries,
    encodings,
    neighbour_ids,
    block_place,
    query_weight,
    key_weight,
    value_weight,
    attn_grad,
):
    dp_count = lax.axis_size("dp")
    own_blocks = encodings.shape[0]
    span_count = neighbour_ids.shape[0]
    block_names = neighbour_ids.reshape(-1)
    slot_count = block_names.shape[0]
    capacity = -(-slot_count // dp_count)
    position = block_place[block_names]
    owner_dev = position // own_blocks
    local_slot = position % own_blocks
    slot_order = jnp.arange(slot_count, dtype=jnp.int32)
    same_owner = (owner_dev[:, None] == owner_dev[None, :]) & (
        slot_order[None, :] < slot_order[:, None]
    )
    slot_rank = jnp.sum(same_owner.astype(jnp.int32), axis=1)
    device_match = owner_dev[:, None, None] == jnp.arange(dp_count, dtype=jnp.int32)[None, :, None]
    rank_match = slot_rank[:, None, None] == jnp.arange(capacity, dtype=jnp.int32)[None, None, :]
    requests = (
        jnp.sum(jnp.where(device_match & rank_match, local_slot[:, None, None] + 1, 0), axis=0) - 1
    )
    asked_rows = lax.all_to_all(requests, "dp", split_axis=0, concat_axis=0, tiled=True)
    valid_mask = asked_rows >= 0
    local_index = jnp.maximum(asked_rows, 0)
    blank = jnp.zeros((), jnp.bfloat16)
    packed = jnp.where(valid_mask[:, :, None, None], encodings[local_index], blank)
    received = lax.all_to_all(packed, "dp", split_axis=0, concat_axis=0, tiled=True)
    slot_blocks = lax.all_gather(received[owner_dev, slot_rank], "head", axis=2, tiled=True)
    flat_rows = slot_blocks.reshape(-1, E)
    both_weights = jnp.concatenate([key_weight, value_weight], axis=1)
    head_cols = key_weight.shape[1]
    local_heads = head_cols // DH
    projected = jnp.dot(flat_rows, both_weights, preferred_element_type=jnp.float32).astype(
        jnp.bfloat16
    )
    key_rows = projected[:, :head_cols].reshape(span_count, NEIGH * NTOK, local_heads, DH)
    value_rows = projected[:, head_cols:].reshape(span_count, NEIGH * NTOK, local_heads, DH)
    query_heads = queries.reshape(span_count, CH, local_heads, DH)
    grad_heads = attn_grad.reshape(span_count, CH, local_heads, DH)
    score_scale = 1.0 / math.sqrt(DH)
    scores = (
        jnp.einsum("cqhd,ckhd->chqk", query_heads, key_rows, preferred_element_type=jnp.float32)
        * score_scale
    )
    shifted = jnp.exp(scores - jnp.max(scores, axis=-1, keepdims=True))
    prob_rows = shifted / jnp.sum(shifted, axis=-1, keepdims=True)
    prob_half = prob_rows.astype(jnp.bfloat16)
    grad_probs = jnp.einsum(
        "cqhd,ckhd->chqk", grad_heads, value_rows, preferred_element_type=jnp.float32
    )
    row_delta = jnp.sum(prob_rows * grad_probs, axis=-1, keepdims=True)
    grad_scores = (prob_rows * (grad_probs - row_delta) * score_scale).astype(jnp.bfloat16)
    value_grad = jnp.einsum(
        "chqk,cqhd->ckhd", prob_half, grad_heads, preferred_element_type=jnp.float32
    ).astype(jnp.bfloat16)
    key_grad = jnp.einsum(
        "chqk,cqhd->ckhd", grad_scores, query_heads, preferred_element_type=jnp.float32
    ).astype(jnp.bfloat16)
    query_grad = jnp.einsum(
        "chqk,ckhd->cqhd", grad_scores, key_rows, preferred_element_type=jnp.float32
    ).astype(jnp.bfloat16)
    partial_input = jnp.dot(
        query_grad.reshape(-1, head_cols), query_weight.T, preferred_element_type=jnp.float32
    )
    query_input_grad = lax.psum_scatter(
        partial_input.astype(jnp.bfloat16), "head", scatter_dimension=1, tiled=True
    )
    both_grads = jnp.concatenate(
        [key_grad.reshape(-1, head_cols), value_grad.reshape(-1, head_cols)], axis=1
    )
    weight_grads = lax.psum_scatter(
        lax.dot_general(
            flat_rows, both_grads, (((0,), (0,)), ((), ())), preferred_element_type=jnp.float32
        ),
        "dp",
        scatter_dimension=0,
        tiled=True,
    )
    slot_partial = jnp.dot(both_grads, both_weights.T, preferred_element_type=jnp.float32).reshape(
        slot_count, NTOK, E
    )
    slot_grad = lax.psum_scatter(
        slot_partial.astype(jnp.bfloat16), "head", scatter_dimension=2, tiled=True
    )
    quarter = slot_grad.shape[2]
    outgoing = (
        jnp.zeros((dp_count, capacity, NTOK, quarter), jnp.bfloat16)
        .at[owner_dev, slot_rank]
        .set(slot_grad)
    )
    returned = lax.all_to_all(outgoing, "dp", split_axis=0, concat_axis=0, tiled=True)
    block_match = (
        local_index.reshape(-1)[None, :] == jnp.arange(own_blocks, dtype=jnp.int32)[:, None]
    )
    target = (block_match & valid_mask.reshape(-1)[None, :]).astype(jnp.bfloat16)
    encodings_grad = jnp.dot(
        target, returned.reshape(dp_count * capacity, -1), preferred_element_type=jnp.float32
    )
    encodings_grad = encodings_grad.reshape(own_blocks, NTOK, quarter).astype(jnp.bfloat16)
    return (
        query_input_grad,
        encodings_grad,
        weight_grads[:, :head_cols],
        weight_grads[:, head_cols:],
    )


def solution(mesh):
    in_specs = (
        P("dp", "head"),
        P("dp", None, "head"),
        P("dp", None),
        P(),
        P(None, "head"),
        P(None, "head"),
        P(None, "head"),
        P("dp", "head"),
    )
    out_specs = (P("dp", "head"), P("dp", None, "head"), P("dp", "head"), P("dp", "head"))
    return jax.shard_map(shards, mesh=mesh, in_specs=in_specs, out_specs=out_specs, check_vma=False)
```

profile of v0, /device:TPU:0, one launch (start us, length us, event | category | flops | bytes accessed | tf_op | source)
XLA Modules:
  0.0 362.5 jit_solution(3672516325718098213)
XLA Ops:
  7.2 0.8 copy.63
  8.1 1.3 gather_fusion
  9.9 13.5 %all_to_all.16 = s32[8,1,2]{2,1,0:T(1,128)S(1)} all-to-all(s32[8,1,2]{2,1,0:T(1,128)S(1)} %copy.64), channel_id=1, replica_groups=mesh['dp'=8,'head'=4] {'dp'}, dimensions={0} | all-to-all | bytes 128 | tf_op jit(solution)/shard_map/all_to_all | solution.py:44
  23.7 0.7 gather_fusion.1
  24.5 1.1 broadcast_select_fusion
  25.5 3.7 %all-to-all-start.1 = ((bf16[8,2,128,224]{2,3,1,0:T(8,128)(2,1)}), bf16[8,2,128,224]{2,3,1,0:T(8,128)(2,1)S(1)}, u32[]{:S(2)}, u32[]{:S(2)}) async-start(bf16[8,2,128,224]{2,3,1,0:T(8,128)(2,1)} %broadcast_select_fusion), calls=%async_computation.1 | async-start | bytes 1835008 | tf_op jit(solution)/shard_map/all_to_all | solution.py:49
  29.3 21.8 %all-to-all-done.1 = bf16[8,2,128,224]{2,3,1,0:T(8,128)(2,1)S(1)} async-done(((bf16[8,2,128,224]{2,3,1,0:T(8,128)(2,1)}), bf16[8,2,128,224]{2,3,1,0:T(8,128)(2,1)S(1)}, u32[]{:S(2)}, u32[]{:S(2)}) %all-to-all-start.1) | async-done | bytes 917536 | tf_op jit(solution)/shard_map/all_to_all | solution.py:49
  51.1 1.6 gather_fusion.2
  53.0 1.2 reshape.289
  54.2 1.0 constant_dynamic-update-slice_fusion.1
  55.3 1.0 constant_dynamic-update-slice_fusion
  56.3 27.0 %all-gather.2.cloned.1.call-done = bf16[16,128,896]{1,2,0:T(8,128)(2,1)} async-done(((bf16[16,128,224]{1,2,0:T(8,128)(2,1)}), bf16[16,128,896]{1,2,0:T(8,128)(2,1)}) %all-gather.2.cloned.1.call-update) | async-done | bytes 3670032 | tf_op jit(solution)/shard_map/all_gather | solution.py:50
  83.3 6.1 %copy.67 = bf16[16,128,896]{2,1,0:T(8,128)(2,1)} copy(bf16[16,128,896]{1,2,0:T(8,128)(2,1)} %all-gather.2.cloned.1.call-done) | data formatting | bytes 7340032 | tf_op jit(solution)/shard_map/all_gather | solution.py:50
  89.4 7.1 %convolution_convert_fusion.1 = bf16[2048,1024]{1,0:T(8,128)(2,1)S(1)} fusion(bf16[2048,896]{1,0:T(8,128)(2,1)} %bitcast.121, bf16[896,1024]{1,0:T(8,128)(2,1)} %constant_dynamic-update-slice_fusion), kind=kOutput, calls=%fused_computation.7 | convolution fusion | flops 3760193536 | bytes 9699328 | tf_op jit(solution)/shard_map/dot_general | solution.py:55
  96.5 1.6 fusion.52
  98.1 2.1 reshape.288
  100.1 2.5 reshape.286
  102.7 0.8 fusion.12
  103.6 1.8 fusion.54
  105.4 0.3 copy-done.3
  105.7 1.0 copy-done.2
  106.7 2.2 fusion.7
  108.8 7.9 %convert_bitcast_fusion = bf16[8,256,4,128]{3,1,2,0:T(8,128)(2,1)} fusion(bf16[8,64,4,128]{3,2,1,0:T(4,128)(2,1)S(1)} %reshape.289, f32[8,4,64]{2,1,0:T(4,128)S(1)} %get-tuple-element.30, f32[8,4,256,64]{2,3,1,0:T(8,128)} %copy-done.3), kind=kOutput, calls=%fused_computation.20 | convolution fusion | flops 137890048 | bytes 4726784 | tf_op jit(solution)/shard_map/chqk,cqhd->ckhd/dot_general | solution.py:75
  116.7 17.0 %convert_bitcast_fusion.1 = bf16[8,256,4,128]{3,1,2,0:T(8,128)(2,1)} fusion(f32[8,4,256,64]{2,3,1,0:T(8,128)} %fusion.7, bf16[8,64,4,128]{3,2,1,0:T(4,128)(2,1)S(1)} %reshape.287, f32[8,4,64,256]{3,2,1,0:T(8,128)} %get-tuple-element.31, f32[8,4,64]{2,1,0:T(4,128)S(1)} %get-tuple-element.30), kind=kOutput, calls=%fused_computation.21 | convolution fusion | flops 138938624 | bytes 6823936 | tf_op jit(solution)/shard_map/chqk,cqhd->ckhd/dot_general | solution.py:78
  133.7 4.5 %copy.75 = bf16[8,256,4,128]{1,0,3,2:T(8,128)(2,1)} copy(bf16[8,256,4,128]{3,1,2,0:T(8,128)(2,1)} %convert_bitcast_fusion.1) | data formatting | bytes 4194304 | tf_op jit(solution)/shard_map/convert_element_type | solution.py:80
  138.2 3.6 copy.83
  141.8 4.5 %copy.77 = bf16[8,256,4,128]{1,0,3,2:T(8,128)(2,1)} copy(bf16[8,256,4,128]{3,1,2,0:T(8,128)(2,1)} %convert_bitcast_fusion) | data formatting | bytes 4194304 | tf_op jit(solution)/shard_map/convert_element_type | solution.py:77
  146.3 2.4 copy.84
  149.0 8.9 %convolution_convert_fusion.2 = bf16[2048,896]{1,0:T(8,128)(2,1)} fusion(bf16[2048,1024]{0,1:T(8,128)(2,1)S(1)} %constant_dynamic-update-slice_fusion.2, bf16[896,1024]{1,0:T(8,128)(2,1)} %constant_dynamic-update-slice_fusion), kind=kOutput, calls=%fused_computation.8 | convolution fusion | flops 3759931392 | bytes 9699328 | tf_op jit(solution)/shard_map/dot_general | solution.py:101
  158.0 6.0 %copy.78 = bf16[16,128,896]{1,2,0:T(8,128)(2,1)} copy(bf16[16,128,896]{2,1,0:T(8,128)(2,1)} %bitcast.123) | data formatting | bytes 7340032 | tf_op jit(solution)/shard_map/convert_element_type | solution.py:105
  164.1 9.3 %fusion.55 = f32[896,1024]{1,0:T(8,128)} fusion(bf16[2048,896]{1,0:T(8,128)(2,1)} %bitcast.122, bf16[2048,1024]{0,1:T(8,128)(2,1)} %copy-done.5), kind=kOutput, calls=%fused_computation.91 | convolution fusion | flops 3758096384 | bytes 11534336 | tf_op jit(solution)/shard_map/dot_general | solution.py:94
  173.4 0.3 reduce-scatter.4.cloned.1.call-start
  173.6 14.9 %fusion.19 = bf16[8,64,4,128]{3,1,2,0:T(8,128)(2,1)S(1)} fusion(bf16[8,256,4,128]{3,2,1,0:T(4,128)(2,1)S(1)} %reshape.286, f32[8,4,256,64]{2,3,1,0:T(8,128)} %fusion.7, f32[8,4,64,256]{3,2,1,0:T(8,128)} %get-tuple-element.31, f32[8,4,64]{2,1,0:T(4,128)S(1)} %get-tuple-element.30), kind=kOutput, calls=%fused_computation.29 | convolution fusion | flops 138152192 | bytes 6823936 | tf_op jit(solution)/shard_map/chqk,ckhd->cqhd/dot_general | solution.py:81
  188.5 0.4 copy.73
  189.0 6.5 %convolution_convert_fusion = bf16[512,4096]{1,0:T(8,128)(2,1)} fusion(bf16[4096,512]{1,0:T(8,128)(2,1)} %param.12, bf16[64,8,4,128]{3,2,1,0:T(4,128)(2,1)S(1)} %bitcast.125), kind=kOutput, calls=%fused_computation.6 | convolution fusion | flops 2149580800 | bytes 8912896 | tf_op jit(solution)/shard_map/dot_general | solution.py:84
  195.5 10.0 %reduce-scatter.6.cloned.1.call-done = bf16[16,128,224]{1,2,0:T(8,128)(2,1)} async-done(((bf16[16,128,896]{1,2,0:T(8,128)(2,1)}), bf16[16,128,224]{1,2,0:T(8,128)(2,1)}) %reduce-scatter.6.cloned.1.call-update) | async-done | bytes 917520 | tf_op jit(solution)/shard_map/reduce_scatter | solution.py:104
  205.5 1.0 broadcast_in_dim.23
  206.5 3.4 scatter_fusion
  210.0 5.6 %all-to-all-start.2 = ((bf16[8,2,128,224]{2,3,1,0:T(8,128)(2,1)}), bf16[8,2,128,224]{2,3,1,0:T(8,128)(2,1)S(1)}, u32[]{:S(2)}, u32[]{:S(2)}) async-start(bf16[8,2,128,224]{2,3,1,0:T(8,128)(2,1)} %scatter_fusion), calls=%async_computation.4 | async-start | bytes 1835008 | tf_op jit(solution)/shard_map/all_to_all | solution.py:113
  215.6 93.0 %reduce-scatter.8.cloned.1.call-done = f32[112,1024]{1,0:T(8,128)} async-done(((f32[896,1024]{1,0:T(8,128)}), f32[112,1024]{1,0:T(8,128)}) %reduce-scatter.8.cloned.1.call-update) | async-done | bytes 458768 | tf_op jit(solution)/shard_map/reduce_scatter | solution.py:93
  308.6 1.8 fusion.53
  310.5 0.5 copy.79
  311.0 1.8 reshape.293
  312.8 1.5 dot_general.46
  314.3 0.8 copy.80
  315.1 0.4 convolution_convert_fusion.3
  315.5 1.2 copy.81
  316.7 39.3 %reduce-scatter.4.cloned.1.call-done = bf16[512,1024]{1,0:T(8,128)(2,1)} async-done(((bf16[512,4096]{1,0:T(8,128)(2,1)}), bf16[512,1024]{1,0:T(8,128)(2,1)}) %reduce-scatter.4.cloned.1.call-update) | async-done | bytes 1048592 | tf_op jit(solution)/shard_map/reduce_scatter | solution.py:87
  (45 shorter events, 1.6 us)
Async XLA Ops:
  7.2 16.6 %copy-start = (bf16[16,128,224]{1,2,0:T(8,128)(2,1)S(1)}, bf16[16,128,224]{1,2,0:T(8,128)(2,1)}, u32[]{:S(2)}) copy-start(bf16[16,128,224]{1,2,0:T(8,128)(2,1)} %param.9) | copy-start | bytes 2752516
  25.5 27.3 %copy-start.8 = (bf16[512,512]{1,0:T(8,128)(2,1)S(1)}, bf16[512,512]{1,0:T(8,128)(2,1)}, u32[]{:S(2)}) copy-start(bf16[512,512]{1,0:T(8,128)(2,1)} %param.8) | copy-start | bytes 1572868
  25.5 25.6 %all-to-all-start.1 = ((bf16[8,2,128,224]{2,3,1,0:T(8,128)(2,1)}), bf16[8,2,128,224]{2,3,1,0:T(8,128)(2,1)S(1)}, u32[]{:S(2)}, u32[]{:S(2)}) async-start(bf16[8,2,128,224]{2,3,1,0:T(8,128)(2,1)} %broadcast_select_fusion), calls=%async_computation.1 | async-start | bytes 1835008 | tf_op jit(solution)/shard_map/all_to_all | solution.py:49
  29.2 54.1 %all-gather.2.cloned.1.call-start = ((), (), s32[]{:S(2)}) async-start(), calls=%async_computation.6 | async-start | bytes 4587520 | tf_op jit(solution)/shard_map/all_gather | solution.py:50
  51.1 3.1 copy-start.6
  52.8 2.5 copy-start.7
  52.8 152.7 %reduce-scatter.6.cloned.1.call-start = ((), (), s32[]{:S(2)}) async-start(), calls=%async_computation.8 | async-start | bytes 4587520 | tf_op jit(solution)/shard_map/reduce_scatter | solution.py:104
  103.5 2.1 copy-start.3
  103.5 3.1 copy-start.2
  146.3 2.4 copy-start.4
  149.0 9.0 %copy-start.5 = (bf16[2048,1024]{0,1:T(8,128)(2,1)}, bf16[2048,1024]{0,1:T(8,128)(2,1)S(1)}, u32[]{:S(2)}) copy-start(bf16[2048,1024]{0,1:T(8,128)(2,1)S(1)} %constant_dynamic-update-slice_fusion.2) | copy-start | bytes 12582916
  164.0 144.6 %reduce-scatter.8.cloned.1.call-start = ((), (), s32[]{:S(2)}) async-start(), calls=%async_computation.9 | async-start | bytes 4128768 | tf_op jit(solution)/shard_map/reduce_scatter | solution.py:93
  173.4 182.6 %reduce-scatter.4.cloned.1.call-start = ((), (), s32[]{:S(2)}) async-start(), calls=%async_computation.7 | async-start | bytes 5242880 | tf_op jit(solution)/shard_map/reduce_scatter | solution.py:87
  210.0 100.5 %all-to-all-start.2 = ((bf16[8,2,128,224]{2,3,1,0:T(8,128)(2,1)}), bf16[8,2,128,224]{2,3,1,0:T(8,128)(2,1)S(1)}, u32[]{:S(2)}, u32[]{:S(2)}) async-start(bf16[8,2,128,224]{2,3,1,0:T(8,128)(2,1)} %scatter_fusion), calls=%async_computation.4 | async-start | bytes 1835008 | tf_op jit(solution)/shard_map/all_to_all | solution.py:113
  314.3 41.7 %copy-start.1 = (bf16[16,128,224]{1,2,0:T(8,128)(2,1)S(1)}, bf16[16,128,224]{1,2,0:T(8,128)(2,1)}, u32[]{:S(2)}) copy-start(bf16[16,128,224]{1,2,0:T(8,128)(2,1)} %param.9) | copy-start | bytes 2752516
Sparse Core Ops, SparseCore 0:
  52.9 30.3 all-gather.1
  164.2 41.2 reduce-scatter.5
  209.6 99.0 reduce-scatter.7
  311.7 44.1 reduce-scatter.3
where the time goes:
time: 364 us; the launch traced here: 363 us
  waiting for transfers between devices  191 us (52%)
  matrix products  75 us (21%)
  local copies, waits for them, and re-layouts  55.8 us (15%)
  between operations  14 us (4%)
  blocking collectives  13.5 us (4%)
  starting transfers between devices  9.66 us (3%)
    reduce_scatter x1, waiting for transfers between devices, shards(): lax.psum_scatter(lax.dot_general(flat_rows, both_grads, (((0,), (0,)), ((...  93 us
    reduce_scatter x1, waiting for transfers between devices, shards(): lax.psum_scatter(partial_input.astype(jnp.bfloat16), 'head', scatter_dime...  39.3 us
    all_gather x1, waiting for transfers between devices, shards(): lax.all_gather(received[owner_dev, slot_rank], 'head', axis=2, tiled=True)  27 us
    all_to_all x1, waiting for transfers between devices, shards(): lax.all_to_all(packed, 'dp', split_axis=0, concat_axis=0, tiled=True)  21.8 us
    dot_general x1, matrix products, shards(): jnp.einsum('chqk,cqhd->ckhd', grad_scores, query_heads, preferred_element...  17 us
    dot_general x1, matrix products, shards(): jnp.einsum('chqk,ckhd->cqhd', grad_scores, key_rows, preferred_element_ty...  14.9 us
    all_to_all x1, blocking collectives, shards(): lax.all_to_all(requests, 'dp', split_axis=0, concat_axis=0, tiled=True)  13.5 us
    unnamed x24, local copies, waits for them, and re-layouts  10.5 us
  transfers between devices with their start and end apart: 6, of which 5 were waited for; matrix products, arithmetic and copies ran while one was open for 13% of the time, Pallas kernels for 0%

commit v1 on v0

--- a/solution.py
+++ b/solution.py
@@ -1,8 +1,11 @@
+import functools
 import math
 
 import jax
 import jax.numpy as jnp
 from jax import lax
+from jax.experimental import pallas as pl
+from jax.experimental.pallas import tpu as pltpu
 from jax.sharding import PartitionSpec as P
 
 DH = 128
@@ -12,7 +15,7 @@
 NEIGH = 2
 
 
-def shards(
+def plain_shards(
     queries,
     encodings,
     neighbour_ids,
@@ -126,6 +129,589 @@
         weight_grads[:, head_cols:],
     )
 
+MESH = pl.DeviceIdType.MESH
+VMEM_LIMIT = 60 * 1024 * 1024
+
+
+def remote(src, dst, send_sem, recv_sem, device):
+    return pltpu.make_async_remote_copy(
+        src_ref=src,
+        dst_ref=dst,
+        send_sem=send_sem,
+        recv_sem=recv_sem,
+        device_id=device,
+        device_id_type=MESH,
+    )
+
+
+def greet(devices):
+    barrier = pltpu.get_barrier_semaphore()
+    for device in devices:
+        pl.semaphore_signal(barrier, inc=1, device_id=device, device_id_type=MESH)
+    pl.semaphore_wait(barrier, len(devices))
+
+
+def places_kernel(n, mine_ref, all_ref, landed, send_sem, recv_sem):
+    me = lax.axis_index("dp")
+    greet([{"dp": lax.rem(me + k, n)} for k in range(1, n)])
+    copies = []
+    for k in range(1, n):
+        copy = remote(
+            mine_ref,
+            landed.at[me],
+            send_sem.at[k - 1],
+            recv_sem.at[k - 1],
+            {"dp": lax.rem(me + k, n)},
+        )
+        copy.start()
+        copies.append(copy)
+    for k in range(1, n):
+        sender = lax.rem(me - k + n, n)
+        remote(
+            mine_ref, landed.at[sender], send_sem.at[k - 1], recv_sem.at[k - 1], {"dp": sender}
+        ).wait_recv()
+        all_ref[sender] = landed[sender]
+    all_ref[me] = mine_ref[...]
+    for copy in copies:
+        copy.wait_send()
+
+
+def gather_kernel(
+    n, packed_ref, out_ref, local_sem, a_send, a_recv, y_send, y_recv, s_send, s_recv, f_send, f_recv
+):
+    me = lax.axis_index("dp")
+    col = lax.axis_index("head")
+    far = lax.rem(col + 2, 4)
+    near = col + 1 - 2 * lax.rem(col, 2)
+    far_near = lax.rem(near + 2, 4)
+    own = pltpu.make_async_copy(packed_ref.at[me], out_ref.at[me, col], local_sem)
+    own.start()
+    greet([{"dp": lax.rem(me + k, n)} for k in range(1, n)] + [{"head": far}, {"head": near}])
+
+    def first(k):
+        return remote(
+            packed_ref.at[lax.rem(me + k, n)],
+            out_ref.at[me, col],
+            a_send.at[k],
+            a_recv.at[k],
+            {"dp": lax.rem(me + k, n)},
+        )
+
+    def arrived(k):
+        sender = lax.rem(me - k + n, n)
+        return remote(
+            packed_ref.at[sender], out_ref.at[sender, col], a_send.at[k], a_recv.at[k], {"dp": sender}
+        )
+
+    def across(k, feature, sems, target):
+        sender = lax.rem(me - k + n, n)
+        block = out_ref.at[sender, feature]
+        return remote(block, block, sems[0].at[k], sems[1].at[k], {"head": target})
+
+    y_sems, s_sems, f_sems = (y_send, y_recv), (s_send, s_recv), (f_send, f_recv)
+    for k in range(1, n):
+        first(k).start()
+    own.wait()
+    for k in range(n):
+        if k:
+            arrived(k).wait_recv()
+        across(k, col, y_sems, far).start()
+        across(k, col, s_sems, near).start()
+    for k in range(n):
+        across(k, far, y_sems, far).wait_recv()
+        across(k, far, f_sems, near).start()
+    for k in range(n):
+        across(k, near, s_sems, near).wait_recv()
+        across(k, far_near, f_sems, near).wait_recv()
+    for k in range(n):
+        if k:
+            first(k).wait_send()
+        across(k, col, y_sems, far).wait_send()
+        across(k, col, s_sems, near).wait_send()
+        across(k, far, f_sems, near).wait_send()
+
+
+def dot(a, b, over_a, over_b):
+    return lax.dot_general(
+        a, b, (((over_a,), (over_b,)), ((), ())), preferred_element_type=jnp.float32
+    )
+
+
+def span_kernel(
+    dev_ref, rank_ref, one_ref, two_ref, q_ref, g_ref, wk_ref, wv_ref, blocks_ref, grads_ref, dq_ref
+):
+    depth = wk_ref.shape[0]
+    cols = wk_ref.shape[1]
+    rows = jnp.concatenate(
+        [one_ref[...].reshape(depth, NTOK), two_ref[...].reshape(depth, NTOK)], axis=1
+    )
+    blocks_ref[...] = rows
+    keys = dot(rows, wk_ref[...], 0, 0).astype(jnp.bfloat16)
+    values = dot(rows, wv_ref[...], 0, 0).astype(jnp.bfloat16)
+    scale = 1.0 / math.sqrt(DH)
+    for head in range(cols // DH):
+        at = slice(head * DH, (head + 1) * DH)
+        q, g, k, v = q_ref[:, at], g_ref[:, at], keys[:, at], values[:, at]
+        scores = dot(q, k, 1, 1) * scale
+        shifted = jnp.exp(scores - jnp.max(scores, axis=-1, keepdims=True))
+        probs = shifted / jnp.sum(shifted, axis=-1, keepdims=True)
+        dprobs = dot(g, v, 1, 1)
+        delta = jnp.sum(probs * dprobs, axis=-1, keepdims=True)
+        dscores = (probs * (dprobs - delta) * scale).astype(jnp.bfloat16)
+        half = probs.astype(jnp.bfloat16)
+        grads_ref[:, at] = dot(dscores, q, 0, 0).astype(jnp.bfloat16)
+        grads_ref[:, cols + head * DH : cols + (head + 1) * DH] = dot(half, g, 0, 0).astype(
+            jnp.bfloat16
+        )
+        dq_ref[:, at] = dot(dscores, k, 1, 0).astype(jnp.bfloat16)
+
+
+def exchange_kernel(
+    n,
+    cap,
+    slot_ref,
+    blocks_hbm,
+    grads_hbm,
+    dq_hbm,
+    qw_hbm,
+    wk_hbm,
+    wv_hbm,
+    qi_ref,
+    ret_ref,
+    kw_ref,
+    vw_ref,
+    blocks,
+    grads,
+    dq,
+    qw,
+    wk,
+    wv,
+    load_sem,
+    s_own,
+    s_out,
+    s_in,
+    s_far,
+    s_far_in,
+    s_sum,
+    s_back,
+    s_back_in,
+    q_own,
+    q_out,
+    q_in,
+    q_far,
+    q_far_in,
+    w_own,
+    w_out,
+    w_in,
+    w_far,
+    w_far_in,
+    ss_sem,
+    sy_sem,
+    a_sem,
+    qs_sem,
+    qy_sem,
+    wx_sem,
+    wz_sem,
+):
+    me = lax.axis_index("dp")
+    col = lax.axis_index("head")
+    high, low = col // 2, lax.rem(col, 2)
+    far = {"head": lax.rem(col + 2, 4)}
+    near = {"head": col + 1 - 2 * low}
+    side, line = lax.rem(me, 2), me // 2
+    lines = n // 2
+    pair = {"dp": me + 1 - 2 * side}
+    loads = [
+        pltpu.make_async_copy(src, dst, load_sem.at[i])
+        for i, (src, dst) in enumerate(
+            [
+                (wk_hbm, wk),
+                (wv_hbm, wv),
+                (grads_hbm, grads),
+                (blocks_hbm, blocks),
+                (dq_hbm, dq),
+                (qw_hbm, qw),
+            ]
+        )
+    ]
+    for load in loads:
+        load.start()
+    greet([{"dp": lax.rem(me + k, n)} for k in range(1, n)] + [far, near])
+    s_groups, quarter, s_cols = s_far.shape
+    cols = wk.shape[1]
+    q_groups, q_rows, q_cols = q_far.shape
+    w_groups, w_rows, w_cols = w_own.shape[0], w_own.shape[2], w_own.shape[3]
+
+    def f32(x):
+        return x.astype(jnp.float32)
+
+    def near_copy(out, landed, sems, i):
+        return remote(out.at[i], landed.at[i], sems.at[0, i], sems.at[1, i], near)
+
+    def far_copy(out, landed, sems, i):
+        return remote(out.at[i], landed.at[i], sems.at[0, i], sems.at[1, i], far)
+
+    def slot_terms(i):
+        at = pl.ds(pl.multiple_of(i * s_cols, s_cols), s_cols)
+        key_rows, value_rows = grads[at, :cols], grads[at, cols:]
+        for part in range(2):
+            for target, owner in ((s_out, 1 - low), (s_own, low)):
+                rows = pl.ds(pl.multiple_of((2 * part + owner) * quarter, 16), quarter)
+                term = dot(wk[rows, :], key_rows, 1, 1) + dot(wv[rows, :], value_rows, 1, 1)
+                target[i, part] = term.astype(jnp.bfloat16)
+        near_copy(s_out, s_in, ss_sem, i).start()
+
+    def slot_pairs(i):
+        near_copy(s_out, s_in, ss_sem, i).wait_recv()
+        s_far[i] = (f32(s_own[i, 1 - high]) + f32(s_in[i, 1 - high])).astype(jnp.bfloat16)
+        far_copy(s_far, s_far_in, sy_sem, i).start()
+
+    def slot_sums(i):
+        far_copy(s_far, s_far_in, sy_sem, i).wait_recv()
+        total = (f32(s_own[i, high]) + f32(s_in[i, high]) + f32(s_far_in[i])).astype(jnp.bfloat16)
+        per = s_cols // NTOK
+        for j in range(per):
+            s_sum[i * per + j] = total[:, j * NTOK : (j + 1) * NTOK]
+
+    def query_terms(i):
+        for part in range(2):
+            for target, owner in ((q_out, 1 - low), (q_own, low)):
+                start = (2 * part + owner) * (q_groups * q_cols) + i * q_cols
+                rows = pl.ds(pl.multiple_of(start, q_cols), q_cols)
+                target[i, part] = dot(dq[...], qw[rows, :], 1, 1).astype(jnp.bfloat16)
+        near_copy(q_out, q_in, qs_sem, i).start()
+
+    def query_pairs(i):
+        near_copy(q_out, q_in, qs_sem, i).wait_recv()
+        q_far[i] = (f32(q_own[i, 1 - high]) + f32(q_in[i, 1 - high])).astype(jnp.bfloat16)
+        far_copy(q_far, q_far_in, qy_sem, i).start()
+
+    def query_sums(i):
+        far_copy(q_far, q_far_in, qy_sem, i).wait_recv()
+        at = pl.ds(pl.multiple_of(i * q_cols, q_cols), q_cols)
+        qi_ref[:, at] = (f32(q_own[i, high]) + f32(q_in[i, high]) + f32(q_far_in[i])).astype(
+            jnp.bfloat16
+        )
+
+    def weight_dot(i, which):
+        at = pl.ds(pl.multiple_of(i * w_cols, w_cols), w_cols)
+        rows = blocks[:, which].reshape(lines * w_rows, blocks.shape[3])
+        return dot(rows, grads[:, at], 1, 0).reshape(lines, w_rows, w_cols)
+
+    def weight_copy(i):
+        return remote(w_out.at[i], w_in.at[i], wx_sem.at[0, i], wx_sem.at[1, i], pair)
+
+    def weight_send(i):
+        w_out[i] = weight_dot(i, 1 - side).astype(jnp.bfloat16)
+        weight_copy(i).start()
+
+    def weight_keep(i):
+        w_own[i] = weight_dot(i, side)
+
+    def line_copy(i, k, sign):
+        there = 2 * lax.rem(line + sign * k + lines, lines) + side
+        return remote(
+            w_far.at[i, k - 1],
+            w_far_in.at[i, k - 1],
+            wz_sem.at[0, i, k - 1],
+            wz_sem.at[1, i, k - 1],
+            {"dp": there},
+        )
+
+    def weight_pairs(i):
+        weight_copy(i).wait_recv()
+        for k in range(1, lines):
+            there = lax.rem(line + k, lines)
+            w_far[i, k - 1] = (w_own[i, there] + f32(w_in[i, there])).astype(jnp.bfloat16)
+            line_copy(i, k, 1).start()
+
+    def weight_sums(i):
+        total = w_own[i, line] + f32(w_in[i, line])
+        for k in range(1, lines):
+            line_copy(i, k, -1).wait_recv()
+            total = total + f32(w_far_in[i, k - 1])
+        return total
+
+    def back_copy(k):
+        return remote(
+            s_back.at[k - 1],
+            s_back_in.at[k - 1],
+            a_sem.at[0, k - 1],
+            a_sem.at[1, k - 1],
+            {"dp": lax.rem(me + k, n)},
+        )
+
+    def loop(start, count, body):
+        def step(i, carry):
+            body(i)
+            return carry
+
+        lax.fori_loop(start, count, step, 0)
+
+    for load in loads[:3]:
+        load.wait()
+    slot_terms(0)
+
+    def slot_step(i):
+        slot_terms(i)
+        slot_pairs(i - 1)
+
+    loop(1, s_groups, slot_step)
+    loads[3].wait()
+    weight_send(0)
+    slot_pairs(s_groups - 1)
+    loop(1, w_groups, weight_send)
+    loads[4].wait()
+    loads[5].wait()
+    query_terms(0)
+
+    def query_step(i):
+        query_terms(i)
+        query_pairs(i - 1)
+
+    loop(1, q_groups, query_step)
+    loop(0, w_groups, weight_keep)
+    query_pairs(q_groups - 1)
+    loop(0, s_groups, slot_sums)
+    for k in range(1, n):
+        there = lax.rem(me + k, n)
+        for r in range(cap):
+            s_back[k - 1, r] = s_sum[slot_ref[there * cap + r]]
+        back_copy(k).start()
+    for r in range(cap):
+        ret_ref[me, r] = s_sum[slot_ref[me * cap + r]]
+    loop(0, w_groups, weight_pairs)
+    loop(0, q_groups, query_sums)
+    for i in range(w_groups):
+        total = weight_sums(i)
+        at = i * w_cols
+        out, at = (kw_ref, at) if at < cols else (vw_ref, at - cols)
+        out[:, at : at + w_cols] = total
+    for k in range(1, n):
+        back_copy(k).wait_recv()
+        ret_ref[lax.rem(me - k + n, n)] = s_back_in[k - 1]
+
+    def sent(i):
+        near_copy(s_out, s_in, ss_sem, i).wait_send()
+        far_copy(s_far, s_far_in, sy_sem, i).wait_send()
+
+    loop(0, s_groups, sent)
+
+    def query_sent(i):
+        near_copy(q_out, q_in, qs_sem, i).wait_send()
+        far_copy(q_far, q_far_in, qy_sem, i).wait_send()
+
+    loop(0, q_groups, query_sent)
+
+    def weight_sent(i):
+        weight_copy(i).wait_send()
+        for k in range(1, lines):
+            line_copy(i, k, 1).wait_send()
+
+    loop(0, w_groups, weight_sent)
+    for k in range(1, n):
+        back_copy(k).wait_send()
+
+
+def scatter_kernel(index_ref, ret_ref, out_ref, total):
+    total[...] = jnp.zeros_like(total)
+    senders, cap = ret_ref.shape[:2]
+
+    def add(i, carry):
+        place = index_ref[i]
+
+        @pl.when(place >= 0)
+        def _():
+            at = jnp.maximum(place, 0)
+            total[at] += ret_ref[i // cap, i % cap].astype(jnp.float32)
+
+        return carry
+
+    lax.fori_loop(0, senders * cap, add, 0)
+
+    def turn(i, carry):
+        out_ref[i] = total[i].T.astype(jnp.bfloat16)
+        return carry
+
+    lax.fori_loop(0, total.shape[0], turn, 0)
+
+
+def call(kernel, out_shape, scratch, collective=None, **kwargs):
+    params = dict(vmem_limit_bytes=VMEM_LIMIT)
+    if collective is not None:
+        params.update(collective_id=collective, has_side_effects=True)
+    return pl.pallas_call(
+        kernel,
+        out_shape=out_shape,
+        scratch_shapes=scratch,
+        compiler_params=pltpu.CompilerParams(**params),
+        **kwargs,
+    )
+
+
+def shards(
+    queries,
+    encodings,
+    neighbour_ids,
+    block_place,
+    query_weight,
+    key_weight,
+    value_weight,
+    attn_grad,
+):
+    n = lax.axis_size("dp")
+    bf16, f32, i32 = jnp.bfloat16, jnp.float32, jnp.int32
+    own_blocks, _, quarter = encodings.shape
+    spans = neighbour_ids.shape[0]
+    slots = spans * NEIGH
+    cap = -(-slots // n)
+    me = lax.axis_index("dp")
+    cols = key_weight.shape[1]
+    depth = key_weight.shape[0]
+    vmem = pl.BlockSpec(memory_space=pltpu.VMEM)
+    anywhere = pl.BlockSpec(memory_space=pl.ANY)
+    dma = pltpu.SemaphoreType.DMA
+    sds = jax.ShapeDtypeStruct
+
+    position = block_place[neighbour_ids.reshape(-1)]
+    padded = jnp.zeros((8, 128), i32).at[0, :slots].set(position)
+    places = call(
+        functools.partial(places_kernel, n),
+        sds((n, 8, 128), i32),
+        [pltpu.VMEM((n, 8, 128), i32), dma((n - 1,)), dma((n - 1,))],
+        collective=0,
+        in_specs=[vmem],
+        out_specs=vmem,
+    )(padded)[:, 0, :slots]
+
+    earlier = jnp.arange(slots, dtype=i32)[None, :] < jnp.arange(slots, dtype=i32)[:, None]
+    ranks = jnp.arange(cap, dtype=i32)
+    mine = (places // own_blocks) == me
+    asked_rank = jnp.sum((mine[:, None, :] & earlier[None]).astype(i32), axis=2)
+    pick = mine[:, None, :] & (asked_rank[:, None, :] == ranks[None, :, None])
+    asked = jnp.sum(jnp.where(pick, (places % own_blocks)[:, None, :] + 1, 0), axis=2) - 1
+    owner = position // own_blocks
+    rank = jnp.sum(((owner[:, None] == owner[None, :]) & earlier).astype(i32), axis=1)
+    chosen = (owner[None, None, :] == jnp.arange(n, dtype=i32)[:, None, None]) & (
+        rank[None, None, :] == ranks[None, :, None]
+    )
+    slot_at = jnp.sum(jnp.where(chosen, jnp.arange(slots, dtype=i32), 0), axis=2).reshape(-1)
+
+    packed = jnp.swapaxes(encodings, 1, 2)[jnp.maximum(asked, 0)]
+    gathered = call(
+        functools.partial(gather_kernel, n),
+        sds((n, 4, cap, quarter, NTOK), bf16),
+        [dma] + [dma((n,))] * 8,
+        collective=1,
+        in_specs=[anywhere],
+        out_specs=anywhere,
+    )(packed)
+
+    def block_spec(j):
+        return pl.BlockSpec(
+            (1, 4, 1, quarter, NTOK),
+            lambda i, dev, order: (dev[NEIGH * i + j], 0, order[NEIGH * i + j], 0, 0),
+        )
+
+    keys = NEIGH * NTOK
+    tokens = spans * keys
+    whole = pl.BlockSpec((depth, cols), lambda i, dev, order: (0, 0))
+    per_span = pl.BlockSpec((CH, cols), lambda i, dev, order: (i, 0))
+    blocks, grads, dq = call(
+        span_kernel,
+        [sds((depth, tokens), bf16), sds((tokens, 2 * cols), bf16), sds((spans * CH, cols), bf16)],
+        (),
+        grid_spec=pltpu.PrefetchScalarGridSpec(
+            num_scalar_prefetch=2,
+            grid=(spans,),
+            in_specs=[block_spec(0), block_spec(1), per_span, per_span, whole, whole],
+            out_specs=[
+                pl.BlockSpec((depth, keys), lambda i, dev, order: (0, i)),
+                pl.BlockSpec((keys, 2 * cols), lambda i, dev, order: (i, 0)),
+                per_span,
+            ],
+        ),
+    )(owner, rank, gathered, gathered, queries, attn_grad, key_weight, value_weight)
+
+    lines, w_rows, groups = n // 2, depth // n, 4
+    s_cols = tokens // groups
+    q_rows = queries.shape[0]
+    q_width = query_weight.shape[0] // 4
+    q_cols = q_width // groups
+    w_cols = 2 * cols // groups
+
+    def buffer(*shape, dtype=bf16):
+        return pltpu.VMEM(shape, dtype)
+
+    scratch = [
+        buffer(lines, 2, w_rows, tokens),
+        buffer(tokens, 2 * cols),
+        buffer(q_rows, cols),
+        buffer(*query_weight.shape),
+        buffer(depth, cols),
+        buffer(depth, cols),
+        dma((6,)),
+        buffer(groups, 2, quarter, s_cols),
+        buffer(groups, 2, quarter, s_cols),
+        buffer(groups, 2, quarter, s_cols),
+        buffer(groups, quarter, s_cols),
+        buffer(groups, quarter, s_cols),
+        buffer(slots, quarter, NTOK),
+        buffer(n - 1, cap, quarter, NTOK),
+        buffer(n - 1, cap, quarter, NTOK),
+        buffer(groups, 2, q_rows, q_cols),
+        buffer(groups, 2, q_rows, q_cols),
+        buffer(groups, 2, q_rows, q_cols),
+        buffer(groups, q_rows, q_cols),
+        buffer(groups, q_rows, q_cols),
+        buffer(groups, lines, w_rows, w_cols, dtype=f32),
+        buffer(groups, lines, w_rows, w_cols),
+        buffer(groups, lines, w_rows, w_cols),
+        buffer(groups, lines - 1, w_rows, w_cols),
+        buffer(groups, lines - 1, w_rows, w_cols),
+        dma((2, groups)),
+        dma((2, groups)),
+        dma((2, n - 1)),
+        dma((2, groups)),
+        dma((2, groups)),
+        dma((2, groups)),
+        dma((2, groups, lines - 1)),
+    ]
+    query_input_grad, returned, key_grad, value_grad = call(
+        functools.partial(exchange_kernel, n, cap),
+        [
+            sds((q_rows, q_width), bf16),
+            sds((n, cap, quarter, NTOK), bf16),
+            sds((w_rows, cols), f32),
+            sds((w_rows, cols), f32),
+        ],
+        scratch,
+        collective=2,
+        in_specs=[pl.BlockSpec(memory_space=pltpu.SMEM)] + [anywhere] * 6,
+        out_specs=[vmem] * 4,
+    )(
+        slot_at,
+        blocks.reshape(lines, 2, w_rows, tokens),
+        grads,
+        dq,
+        query_weight,
+        key_weight,
+        value_weight,
+    )
+    encodings_grad = call(
+        scatter_kernel,
+        sds(encodings.shape, bf16),
+        [pltpu.VMEM((own_blocks, quarter, NTOK), f32)],
+        in_specs=[pl.BlockSpec(memory_space=pltpu.SMEM), vmem],
+        out_specs=vmem,
+    )(asked.reshape(-1), returned)
+    return query_input_grad, encodings_grad, key_grad, value_grad
+
+
+def fits(mesh):
+    dp, head = mesh.shape["dp"], mesh.shape["head"]
+    return head == 4 and dp % 2 == 0 and dp > 2 and E % (16 * dp) == 0
+
 
 def solution(mesh):
     in_specs = (
@@ -139,4 +725,10 @@
         P("dp", "head"),
     )
     out_specs = (P("dp", "head"), P("dp", None, "head"), P("dp", "head"), P("dp", "head"))
-    return jax.shard_map(shards, mesh=mesh, in_specs=in_specs, out_specs=out_specs, check_vma=False)
+    return jax.shard_map(
+        shards if fits(mesh) else plain_shards,
+        mesh=mesh,
+        in_specs=in_specs,
+        out_specs=out_specs,
+        check_vma=False,
+    )

time: 364 us -> 158 us (0.43)
  waiting for transfers between devices: 191 us -> 0 us
  Pallas kernels: 0 us -> 144 us
  matrix products: 75 us -> 0 us
  local copies, waits for them, and re-layouts: 55.8 us -> 11.6 us
  blocking collectives: 13.5 us -> 0 us
  between operations: 14 us -> 0.77 us
  starting transfers between devices: 9.66 us -> 0 us
    pallas_call x0 -> x5, Pallas kernels: none -> 144 us  [the longest x1 72.9 us: shards(): call(functools.partial(exchange_kernel, n, cap), [sds((q_rows, q_width),...]
    reduce_scatter x3 -> x0, waiting for transfers between devices: 142 us -> none  [the longest x1 93 us: shards(): lax.psum_scatter(lax.dot_general(flat_rows, both_grads, (((0,), (0,)), ((...]
    dot_general x10 -> x0, matrix products: 75 us -> none  [the longest x1 17 us: shards(): jnp.einsum('chqk,cqhd->ckhd', grad_scores, query_heads, preferred_element...]
    all_gather x1 -> x0, waiting for transfers between devices: 27 us -> none  [shards(): lax.all_gather(received[owner_dev, slot_rank], 'head', axis=2, tiled=True)]
    all_to_all x2 -> x0, waiting for transfers between devices: 21.8 us -> none  [the longest x1 21.8 us: shards(): lax.all_to_all(packed, 'dp', split_axis=0, concat_axis=0, tiled=True)]
    convert_element_type x4 -> x0, local copies, waits for them, and re-layouts: 15.5 us -> none  [the longest x1 6.04 us: shards(): slot_partial.astype(jnp.bfloat16)]
    all_to_all x1 -> x0, blocking collectives: 13.5 us -> none  [shards(): lax.all_to_all(requests, 'dp', split_axis=0, concat_axis=0, tiled=True)]
    all_to_all x2 -> x0, starting transfers between devices: 9.27 us -> none  [the longest x1 5.59 us: shards(): lax.all_to_all(outgoing, 'dp', split_axis=0, concat_axis=0, tiled=True)]
  transfers between devices with their start and end apart: 6 -> 0, of which waited for: 5 -> 0; matrix products, arithmetic and copies ran while one was open for 13% -> 0% of each run, Pallas kernels for 0% -> 0%
where the time goes in v1:
time: 158 us
  Pallas kernels  144 us (91%)
  local copies, waits for them, and re-layouts  11.6 us (7%)
    pallas_call x1, Pallas kernels, shards(): call(functools.partial(exchange_kernel, n, cap), [sds((q_rows, q_width),...  72.9 us
    pallas_call x1, Pallas kernels, shards(): call(functools.partial(gather_kernel, n), sds((n, 4, cap, quarter, NTOK),...  32.7 us
    pallas_call x1, Pallas kernels, shards(): call(span_kernel, [sds((depth, tokens), bf16), sds((tokens, 2 * cols), bf...  23.9 us
    pallas_call x1, Pallas kernels, shards(): call(functools.partial(places_kernel, n), sds((n, 8, 128), i32), [pltpu.V...  9.73 us
    unnamed x18, local copies, waits for them, and re-layouts  6.53 us
    pallas_call x1, Pallas kernels, shards(): call(scatter_kernel, sds(encodings.shape, bf16), [pltpu.VMEM((own_blocks,...  4.51 us

profile of v1, /device:TPU:0, one launch (start us, length us, event | category | flops | bytes accessed | tf_op | source)
XLA Modules:
  0.0 157.7 jit_solution(11788959089860893198)
XLA Ops:
  0.6 0.0 copy-start
  0.6 1.2 copy-done
  1.8 0.8 copy.16
  2.6 0.1 reshape.205
  2.7 1.3 gather_fusion
  4.0 0.0 copy-start.4
  4.0 0.2 convert_reduce_fusion.1.rank_ref
  4.2 0.0 copy-start.5
  4.2 0.1 select_reduce_fusion.1
  4.4 0.1 copy.17
  4.5 0.6 reshape.206.slot_ref
  5.1 0.6 scatter.4.mine_ref
  5.7 9.7 %shard_map.111 = s32[8,8,128]{2,1,0:T(8,128)} custom-call(s32[8,128]{1,0:T(8,128)} %scatter.4.mine_ref), custom_call_target="tpu_custom_call" | custom-call | tf_op jit(solution)/shard_map/pallas_call | solution.py:578
  15.4 0.8 fusion.2
  16.2 0.2 convert_reduce_fusion
  16.4 0.1 select_reduce_fusion
  16.6 0.1 copy.19
  16.7 0.6 sub.18.index_ref
  17.3 0.1 copy.18
  17.4 0.1 reshape.219
  17.5 1.6 %gather_fusion.1 = bf16[16,224,128]{2,1,0:T(8,128)(2,1)} fusion(bf16[16,224,128]{2,1,0:T(8,128)(2,1)S(1)} %bitcast.10, s32[1024]{0:T(1024)S(1)} %pad_clamp_fusion), kind=kCustom, calls=%fused_computation.1 | custom fusion | bytes 1835072 | tf_op jit(solution)/shard_map/gather | solution.py:600
  19.0 32.7 %shard_map.112.one_ref.two_ref = bf16[8,4,2,224,128]{4,3,2,1,0:T(8,128)(2,1)} custom-call(bf16[8,2,224,128]{3,2,1,0:T(8,128)(2,1)} %bitcast.12), custom_call_target="tpu_custom_call" | custom-call | tf_op jit(solution)/shard_map/pallas_call | solution.py:601
  51.8 0.0 copy-done.4
  51.8 0.0 copy-done.5
  51.8 23.9 %shard_map.113 = (bf16[896,2048]{1,0:T(8,128)(2,1)}, bf16[2048,1024]{1,0:T(8,128)(2,1)}, bf16[512,512]{1,0:T(8,128)(2,1)}) custom-call(s32[16]{0:T(128)} %copy-done.4, s32[16]{0:T(128)} %copy-done.5, bf16[8,4,2,224,128]{4,3,2,1,0:T(8,128)(2,1)} %shard_map.112.one_ref.two_ref, bf16[8,4,2,224,128]{4,3,2,1,0:T(8,128)(2,1)} %shard_map.112.one_ref.two_ref, ...), custom_call_target="tpu_custom_call" | custom-call | tf_op jit(solution)/shard_map/pallas_call | solution.py:620
  75.7 72.9 %shard_map.114 = (bf16[512,1024]{1,0:T(8,128)(2,1)}, bf16[8,2,224,128]{3,2,1,0:T(8,128)(2,1)}, f32[112,512]{1,0:T(8,128)}, f32[112,512]{1,0:T(8,128)}) custom-call(s32[16]{0:T(128)} %reshape.206.slot_ref, bf16[4,2,112,2048]{3,2,1,0:T(8,128)(2,1)} %bitcast.11, bf16[2048,1024]{1,0:T(8,128)(2,1)} %get-tuple-element.24.grads_hbm, ...), custom_call_target="tpu_custom_call" | custom-call | tf_op jit(solution)/shard_map/pallas_call | solution.py:680
  148.6 0.0 copy-start.1
  148.6 0.0 copy-start.3
  148.6 0.0 copy-start.2
  148.6 4.5 %shard_map.115 = bf16[16,128,224]{2,1,0:T(8,128)(2,1)} custom-call(s32[16]{0:T(128)} %sub.18.index_ref, bf16[8,2,224,128]{3,2,1,0:T(8,128)(2,1)} %get-tuple-element.27.ret_ref), custom_call_target="tpu_custom_call" | custom-call | tf_op jit(solution)/shard_map/pallas_call | solution.py:701
  153.1 2.2 %copy.20 = bf16[16,128,224]{1,2,0:T(8,128)(2,1)} copy(bf16[16,128,224]{2,1,0:T(8,128)(2,1)} %shard_map.115) | data formatting | bytes 1835008
  155.3 0.0 copy-done.1
  155.3 1.0 copy.27
  156.3 0.0 copy-done.3
  156.3 0.7 copy.28
  157.0 0.0 copy-done.2
  157.0 0.7 copy.29
  (10 shorter events, 0.1 us)
Async XLA Ops:
  0.6 1.2 copy-start
  4.0 47.8 %copy-start.4 = (s32[16]{0:T(128)}, s32[16]{0:T(128)S(1)}, u32[]{:S(2)}) copy-start(s32[16]{0:T(128)S(1)} %and_select_fusion.2.dev_ref) | copy-start | bytes 196
  4.2 47.6 %copy-start.5 = (s32[16]{0:T(128)}, s32[16]{0:T(128)S(1)}, u32[]{:S(2)}) copy-start(s32[16]{0:T(128)S(1)} %convert_reduce_fusion.1.rank_ref) | copy-start | bytes 196
  148.6 6.8 %copy-start.1 = (bf16[512,1024]{1,0:T(8,128)(2,1)S(1)}, bf16[512,1024]{1,0:T(8,128)(2,1)}, u32[]{:S(2)}) copy-start(bf16[512,1024]{1,0:T(8,128)(2,1)} %get-tuple-element.50) | copy-start | bytes 3145732
  148.6 7.7 %copy-start.3 = (f32[112,512]{1,0:T(8,128)S(1)}, f32[112,512]{1,0:T(8,128)}, u32[]{:S(2)}) copy-start(f32[112,512]{1,0:T(8,128)} %get-tuple-element.52) | copy-start | bytes 688132
  148.6 8.4 %copy-start.2 = (f32[112,512]{1,0:T(8,128)S(1)}, f32[112,512]{1,0:T(8,128)}, u32[]{:S(2)}) copy-start(f32[112,512]{1,0:T(8,128)} %get-tuple-element.53) | copy-start | bytes 688132

commit v2 on v1

--- a/solution.py
+++ b/solution.py
@@ -176,59 +176,75 @@
         copy.wait_send()
 
 
-def gather_kernel(
-    n, packed_ref, out_ref, local_sem, a_send, a_recv, y_send, y_recv, s_send, s_recv, f_send, f_recv
-):
+def gather_steps(n, packed, got, local_sem, a_sem, y_sem, s_sem, f_sem, ready, project):
     me = lax.axis_index("dp")
     col = lax.axis_index("head")
     far = lax.rem(col + 2, 4)
     near = col + 1 - 2 * lax.rem(col, 2)
     far_near = lax.rem(near + 2, 4)
-    own = pltpu.make_async_copy(packed_ref.at[me], out_ref.at[me, col], local_sem)
-    own.start()
-    greet([{"dp": lax.rem(me + k, n)} for k in range(1, n)] + [{"head": far}, {"head": near}])
+    ahead = 3
 
     def first(k):
+        there = lax.rem(me + k, n)
         return remote(
-            packed_ref.at[lax.rem(me + k, n)],
-            out_ref.at[me, col],
-            a_send.at[k],
-            a_recv.at[k],
-            {"dp": lax.rem(me + k, n)},
+            packed.at[there], got.at[me, col], a_sem.at[0, k], a_sem.at[1, k], {"dp": there}
         )
 
     def arrived(k):
         sender = lax.rem(me - k + n, n)
         return remote(
-            packed_ref.at[sender], out_ref.at[sender, col], a_send.at[k], a_recv.at[k], {"dp": sender}
+            packed.at[sender], got.at[sender, col], a_sem.at[0, k], a_sem.at[1, k], {"dp": sender}
         )
 
     def across(k, feature, sems, target):
-        sender = lax.rem(me - k + n, n)
-        block = out_ref.at[sender, feature]
-        return remote(block, block, sems[0].at[k], sems[1].at[k], {"head": target})
-
-    y_sems, s_sems, f_sems = (y_send, y_recv), (s_send, s_recv), (f_send, f_recv)
-    for k in range(1, n):
+        block = got.at[lax.rem(me - k + n, n), feature]
+        return remote(block, block, sems.at[0, k], sems.at[1, k], {"head": target})
+
+    own = pltpu.make_async_copy(packed.at[me], got.at[me, col], local_sem)
+    own.start()
+    for k in range(1, min(n, 1 + ahead)):
         first(k).start()
     own.wait()
-    for k in range(n):
-        if k:
-            arrived(k).wait_recv()
-        across(k, col, y_sems, far).start()
-        across(k, col, s_sems, near).start()
-    for k in range(n):
-        across(k, far, y_sems, far).wait_recv()
-        across(k, far, f_sems, near).start()
-    for k in range(n):
-        across(k, near, s_sems, near).wait_recv()
-        across(k, far_near, f_sems, near).wait_recv()
-    for k in range(n):
-        if k:
-            first(k).wait_send()
-        across(k, col, y_sems, far).wait_send()
-        across(k, col, s_sems, near).wait_send()
-        across(k, far, f_sems, near).wait_send()
+
+    def spread(k):
+        across(k, col, y_sem, far).start()
+        across(k, col, s_sem, near).start()
+
+    def pass_on(k):
+        across(k, far, y_sem, far).wait_recv()
+        across(k, far, f_sem, near).start()
+
+    def take(k):
+        across(k, near, s_sem, near).wait_recv()
+        across(k, far_near, f_sem, near).wait_recv()
+        project(lax.rem(me - k + n, n))
+
+    spread(0)
+    for k in range(1, n):
+        arrived(k).wait_recv()
+        spread(k)
+        if k + ahead < n:
+            first(k + ahead).start()
+    pass_on(0)
+    ready()
+
+    def step(k, carry):
+        pass_on(k)
+        take(k - 1)
+        return carry
+
+    lax.fori_loop(1, n, step, 0)
+    take(n - 1)
+
+    def finish():
+        for k in range(n):
+            if k:
+                first(k).wait_send()
+            across(k, col, y_sem, far).wait_send()
+            across(k, col, s_sem, near).wait_send()
+            across(k, far, f_sem, near).wait_send()
+
+    return finish
 
 
 def dot(a, b, over_a, over_b):
@@ -237,42 +253,15 @@
     )
 
 
-def span_kernel(
-    dev_ref, rank_ref, one_ref, two_ref, q_ref, g_ref, wk_ref, wv_ref, blocks_ref, grads_ref, dq_ref
-):
-    depth = wk_ref.shape[0]
-    cols = wk_ref.shape[1]
-    rows = jnp.concatenate(
-        [one_ref[...].reshape(depth, NTOK), two_ref[...].reshape(depth, NTOK)], axis=1
-    )
-    blocks_ref[...] = rows
-    keys = dot(rows, wk_ref[...], 0, 0).astype(jnp.bfloat16)
-    values = dot(rows, wv_ref[...], 0, 0).astype(jnp.bfloat16)
-    scale = 1.0 / math.sqrt(DH)
-    for head in range(cols // DH):
-        at = slice(head * DH, (head + 1) * DH)
-        q, g, k, v = q_ref[:, at], g_ref[:, at], keys[:, at], values[:, at]
-        scores = dot(q, k, 1, 1) * scale
-        shifted = jnp.exp(scores - jnp.max(scores, axis=-1, keepdims=True))
-        probs = shifted / jnp.sum(shifted, axis=-1, keepdims=True)
-        dprobs = dot(g, v, 1, 1)
-        delta = jnp.sum(probs * dprobs, axis=-1, keepdims=True)
-        dscores = (probs * (dprobs - delta) * scale).astype(jnp.bfloat16)
-        half = probs.astype(jnp.bfloat16)
-        grads_ref[:, at] = dot(dscores, q, 0, 0).astype(jnp.bfloat16)
-        grads_ref[:, cols + head * DH : cols + (head + 1) * DH] = dot(half, g, 0, 0).astype(
-            jnp.bfloat16
-        )
-        dq_ref[:, at] = dot(dscores, k, 1, 0).astype(jnp.bfloat16)
-
-
 def exchange_kernel(
     n,
     cap,
+    dev_ref,
+    rank_ref,
     slot_ref,
-    blocks_hbm,
-    grads_hbm,
-    dq_hbm,
+    packed_hbm,
+    q_hbm,
+    g_hbm,
     qw_hbm,
     wk_hbm,
     wv_hbm,
@@ -280,13 +269,22 @@
     ret_ref,
     kw_ref,
     vw_ref,
+    got,
+    kv,
     blocks,
     grads,
     dq,
+    q,
+    g,
     qw,
     wk,
     wv,
     load_sem,
+    local_sem,
+    ga_sem,
+    gy_sem,
+    gs_sem,
+    gf_sem,
     s_own,
     s_out,
     s_in,
@@ -327,9 +325,8 @@
             [
                 (wk_hbm, wk),
                 (wv_hbm, wv),
-                (grads_hbm, grads),
-                (blocks_hbm, blocks),
-                (dq_hbm, dq),
+                (q_hbm, q),
+                (g_hbm, g),
                 (qw_hbm, qw),
             ]
         )
@@ -344,6 +341,56 @@
 
     def f32(x):
         return x.astype(jnp.float32)
+
+    def project(sender):
+        rows = jnp.concatenate(
+            [got[sender, :, r].reshape(wk.shape[0], NTOK) for r in range(cap)], axis=1
+        )
+        kv[sender, :, :, :cols] = (
+            dot(rows, wk[...], 0, 0).astype(jnp.bfloat16).reshape(cap, NTOK, cols)
+        )
+        kv[sender, :, :, cols:] = (
+            dot(rows, wv[...], 0, 0).astype(jnp.bfloat16).reshape(cap, NTOK, cols)
+        )
+
+    def weights_ready():
+        for load in loads[:2]:
+            load.wait()
+
+    gather_sent = gather_steps(
+        n, packed_hbm, got, local_sem, ga_sem, gy_sem, gs_sem, gf_sem, weights_ready, project
+    )
+    for load in loads[2:]:
+        load.wait()
+
+    def span(c):
+        places = [(dev_ref[NEIGH * c + j], rank_ref[NEIGH * c + j]) for j in range(NEIGH)]
+        keys = NEIGH * NTOK
+        for j, (dev, rank) in enumerate(places):
+            at = pl.ds(pl.multiple_of(c * keys + j * NTOK, NTOK), NTOK)
+            blocks[:, :, :, at] = got[dev, :, rank].reshape(lines, 2, -1, NTOK)
+        both = jnp.concatenate([kv[dev, rank] for dev, rank in places], axis=0)
+        token_at = pl.ds(pl.multiple_of(c * CH, CH), CH)
+        key_at = pl.ds(pl.multiple_of(c * keys, keys), keys)
+        heads = [slice(h * DH, (h + 1) * DH) for h in range(cols // DH)]
+        q_rows, g_rows = q[token_at, :], g[token_at, :]
+        k_rows, v_rows = both[:, :cols], both[:, cols:]
+        scale = 1.0 / math.sqrt(DH)
+        scores = jnp.concatenate([dot(q_rows[:, at], k_rows[:, at], 1, 1) for at in heads], axis=0)
+        dprobs = jnp.concatenate([dot(g_rows[:, at], v_rows[:, at], 1, 1) for at in heads], axis=0)
+        scores = scores * scale
+        shifted = jnp.exp(scores - jnp.max(scores, axis=-1, keepdims=True))
+        probs = shifted * (1.0 / jnp.sum(shifted, axis=-1, keepdims=True))
+        delta = jnp.sum(probs * dprobs, axis=-1, keepdims=True)
+        dscores = (probs * (dprobs - delta) * scale).astype(jnp.bfloat16)
+        half = probs.astype(jnp.bfloat16)
+        for h, at in enumerate(heads):
+            rows = slice(h * CH, (h + 1) * CH)
+            grads[key_at, at] = dot(dscores[rows], q_rows[:, at], 0, 0).astype(jnp.bfloat16)
+            grads[key_at, cols + at.start : cols + at.stop] = dot(
+                half[rows], g_rows[:, at], 0, 0
+            ).astype(jnp.bfloat16)
+            dq[token_at, at] = dot(dscores[rows], k_rows[:, at], 1, 0).astype(jnp.bfloat16)
 
     def near_copy(out, landed, sems, i):
         return remote(out.at[i], landed.at[i], sems.at[0, i], sems.at[1, i], near)
@@ -448,21 +495,20 @@
 
         lax.fori_loop(start, count, step, 0)
 
-    for load in loads[:3]:
-        load.wait()
-    slot_terms(0)
-
-    def slot_step(i):
+    per_group = s_cols // (NEIGH * NTOK)
+
+    def group(i):
+        loop(i * per_group, (i + 1) * per_group, span)
         slot_terms(i)
+
+    def group_step(i):
+        group(i)
         slot_pairs(i - 1)
 
-    loop(1, s_groups, slot_step)
-    loads[3].wait()
-    weight_send(0)
+    group(0)
+    loop(1, s_groups, group_step)
+    loop(0, w_groups, weight_send)
     slot_pairs(s_groups - 1)
-    loop(1, w_groups, weight_send)
-    loads[4].wait()
-    loads[5].wait()
     query_terms(0)
 
     def query_step(i):
@@ -511,6 +557,7 @@
     loop(0, w_groups, weight_sent)
     for k in range(1, n):
         back_copy(k).wait_send()
+    gather_sent()
 
 
 def scatter_kernel(index_ref, ret_ref, out_ref, total):
@@ -530,7 +577,7 @@
     lax.fori_loop(0, senders * cap, add, 0)
 
     def turn(i, carry):
-        out_ref[i] = total[i].T.astype(jnp.bfloat16)
+        out_ref[i] = total[i].astype(jnp.bfloat16)
         return carry
 
     lax.fori_loop(0, total.shape[0], turn, 0)
@@ -598,41 +645,7 @@
     slot_at = jnp.sum(jnp.where(chosen, jnp.arange(slots, dtype=i32), 0), axis=2).reshape(-1)
 
     packed = jnp.swapaxes(encodings, 1, 2)[jnp.maximum(asked, 0)]
-    gathered = call(
-        functools.partial(gather_kernel, n),
-        sds((n, 4, cap, quarter, NTOK), bf16),
-        [dma] + [dma((n,))] * 8,
-        collective=1,
-        in_specs=[anywhere],
-        out_specs=anywhere,
-    )(packed)
-
-    def block_spec(j):
-        return pl.BlockSpec(
-            (1, 4, 1, quarter, NTOK),
-            lambda i, dev, order: (dev[NEIGH * i + j], 0, order[NEIGH * i + j], 0, 0),
-        )
-
-    keys = NEIGH * NTOK
-    tokens = spans * keys
-    whole = pl.BlockSpec((depth, cols), lambda i, dev, order: (0, 0))
-    per_span = pl.BlockSpec((CH, cols), lambda i, dev, order: (i, 0))
-    blocks, grads, dq = call(
-        span_kernel,
-        [sds((depth, tokens), bf16), sds((tokens, 2 * cols), bf16), sds((spans * CH, cols), bf16)],
-        (),
-        grid_spec=pltpu.PrefetchScalarGridSpec(
-            num_scalar_prefetch=2,
-            grid=(spans,),
-            in_specs=[block_spec(0), block_spec(1), per_span, per_span, whole, whole],
-            out_specs=[
-                pl.BlockSpec((depth, keys), lambda i, dev, order: (0, i)),
-                pl.BlockSpec((keys, 2 * cols), lambda i, dev, order: (i, 0)),
-                per_span,
-            ],
-        ),
-    )(owner, rank, gathered, gathered, queries, attn_grad, key_weight, value_weight)
-
+    tokens = slots * NTOK
     lines, w_rows, groups = n // 2, depth // n, 4
     s_cols = tokens // groups
     q_rows = queries.shape[0]
@@ -644,13 +657,22 @@
         return pltpu.VMEM(shape, dtype)
 
     scratch = [
+        buffer(n, 4, cap, quarter, NTOK),
+        buffer(n, cap, NTOK, 2 * cols),
         buffer(lines, 2, w_rows, tokens),
         buffer(tokens, 2 * cols),
+        buffer(q_rows, cols),
+        buffer(q_rows, cols),
         buffer(q_rows, cols),
         buffer(*query_weight.shape),
         buffer(depth, cols),
         buffer(depth, cols),
-        dma((6,)),
+        dma((5,)),
+        dma,
+        dma((2, n)),
+        dma((2, n)),
+        dma((2, n)),
+        dma((2, n)),
         buffer(groups, 2, quarter, s_cols),
         buffer(groups, 2, quarter, s_cols),
         buffer(groups, 2, quarter, s_cols),
@@ -686,26 +708,28 @@
             sds((w_rows, cols), f32),
         ],
         scratch,
-        collective=2,
-        in_specs=[pl.BlockSpec(memory_space=pltpu.SMEM)] + [anywhere] * 6,
+        collective=1,
+        in_specs=[pl.BlockSpec(memory_space=pltpu.SMEM)] * 3 + [anywhere] * 6,
         out_specs=[vmem] * 4,
     )(
+        owner,
+        rank,
         slot_at,
-        blocks.reshape(lines, 2, w_rows, tokens),
-        grads,
-        dq,
+        packed,
+        queries,
+        attn_grad,
         query_weight,
         key_weight,
         value_weight,
     )
     encodings_grad = call(
         scatter_kernel,
-        sds(encodings.shape, bf16),
+        sds((own_blocks, quarter, NTOK), bf16),
         [pltpu.VMEM((own_blocks, quarter, NTOK), f32)],
         in_specs=[pl.BlockSpec(memory_space=pltpu.SMEM), vmem],
         out_specs=vmem,
     )(asked.reshape(-1), returned)
-    return query_input_grad, encodings_grad, key_grad, value_grad
+    return query_input_grad, jnp.swapaxes(encodings_grad, 1, 2), key_grad, value_grad
 
 
 def fits(mesh):

time: 158 us -> 135 us (0.85)
  Pallas kernels: 144 us -> 121 us
    pallas_call x3 -> x1, Pallas kernels: 61.1 us -> 2.85 us  [shards(): call(scatter_kernel, sds((own_blocks, quarter, NTOK), bf16), [pltpu.VMEM(...]
    pallas_call x1, Pallas kernels: 72.9 us -> 109 us  [shards(): call(functools.partial(exchange_kernel, n, cap), [sds((q_rows, q_width),...]
    unnamed x18 -> x13, local copies, waits for them, and re-layouts: 6.53 us -> 5.45 us
where the time goes in v2:
time: 135 us; the launch traced here: 134 us
  Pallas kernels  121 us (90%)
  local copies, waits for them, and re-layouts  10.6 us (8%)
  other arithmetic  1.54 us (1%)
    pallas_call x1, Pallas kernels, shards(): call(functools.partial(exchange_kernel, n, cap), [sds((q_rows, q_width),...  109 us
    pallas_call x1, Pallas kernels, shards(): call(functools.partial(places_kernel, n), sds((n, 8, 128), i32), [pltpu.V...  9.73 us
    unnamed x13, local copies, waits for them, and re-layouts  5.45 us
    pallas_call x1, Pallas kernels, shards(): call(scatter_kernel, sds((own_blocks, quarter, NTOK), bf16), [pltpu.VMEM(...  2.85 us

profile of v2, /device:TPU:0, one launch (start us, length us, event | category | flops | bytes accessed | tf_op | source)
XLA Modules:
  0.0 134.2 jit_solution(11036507877983804462)
XLA Ops:
  0.6 0.0 copy-start
  0.6 0.8 copy.14
  1.5 0.1 reshape.202
  1.6 1.3 gather_fusion
  2.9 0.6 scatter.4.mine_ref
  3.5 9.7 %shard_map.111 = s32[8,8,128]{2,1,0:T(8,128)} custom-call(s32[8,128]{1,0:T(8,128)} %scatter.4.mine_ref), custom_call_target="tpu_custom_call" | custom-call | tf_op jit(solution)/shard_map/pallas_call | solution.py:625
  13.2 0.8 fusion.2
  14.1 0.2 convert_reduce_fusion
  14.3 0.1 select_reduce_fusion
  14.5 0.1 copy.16
  14.5 0.1 reshape.215
  14.6 0.0 copy-done
  14.6 1.6 %gather_fusion.1 = bf16[16,224,128]{2,1,0:T(8,128)(2,1)} fusion(bf16[16,224,128]{2,1,0:T(8,128)(2,1)S(1)} %bitcast.10, s32[1024]{0:T(1024)S(1)} %pad_clamp_fusion), kind=kCustom, calls=%fused_computation.1 | custom fusion | bytes 1835072 | tf_op jit(solution)/shard_map/gather | solution.py:647
  16.2 0.0 copy-start.2
  16.3 0.2 convert_reduce_fusion.1.rank_ref
  16.4 0.0 copy-start.3
  16.5 0.1 select_reduce_fusion.1
  16.6 0.1 copy.15
  16.7 0.6 reshape.203.slot_ref
  17.3 0.0 copy-done.2
  17.3 0.0 copy-done.3
  17.3 108.8 %shard_map.112 = (bf16[512,1024]{1,0:T(8,128)(2,1)}, bf16[8,2,224,128]{3,2,1,0:T(8,128)(2,1)}, f32[112,512]{1,0:T(8,128)}, f32[112,512]{1,0:T(8,128)}) custom-call(s32[16]{0:T(128)} %copy-done.2, s32[16]{0:T(128)} %copy-done.3, s32[16]{0:T(128)} %reshape.203.slot_ref, bf16[8,2,224,128]{3,2,1,0:T(8,128)(2,1)} %bitcast.11, bf16[512,512]{1,0:T(8,128)(2,1)} %q_hbm.1, ...), custom_call_target="tpu_custom_call" | custom-call | tf_op jit(solution)/shard_map/pallas_call | solution.py:702
  126.1 0.0 copy-start.1
  126.1 0.1 copy.17
  126.2 0.6 sub.18.index_ref
  126.8 2.8 %shard_map.113 = bf16[16,224,128]{2,1,0:T(8,128)(2,1)} custom-call(s32[16]{0:T(128)} %sub.18.index_ref, bf16[8,2,224,128]{3,2,1,0:T(8,128)(2,1)} %get-tuple-element.21.ret_ref), custom_call_target="tpu_custom_call" | custom-call | tf_op jit(solution)/shard_map/pallas_call | solution.py:725
  129.6 2.3 %copy.24 = bf16[512,1024]{1,0:T(8,128)(2,1)} copy(bf16[512,1024]{1,0:T(8,128)(2,1)} %get-tuple-element.32) | data formatting | bytes 2097152
  131.9 1.6 %copy.25 = f32[112,512]{1,0:T(8,128)} copy(f32[112,512]{1,0:T(8,128)} %get-tuple-element.34) | data formatting | bytes 458752
  133.5 0.0 copy-done.1
  133.5 0.7 copy.26
  (10 shorter events, 0.1 us)
Async XLA Ops:
  0.6 14.0 %copy-start = (bf16[16,128,224]{1,2,0:T(8,128)(2,1)S(1)}, bf16[16,128,224]{1,2,0:T(8,128)(2,1)}, u32[]{:S(2)}) copy-start(bf16[16,128,224]{1,2,0:T(8,128)(2,1)} %param.11) | copy-start | bytes 2752516
  16.2 1.1 copy-start.2
  16.4 0.9 copy-start.3
  126.1 7.4 %copy-start.1 = (f32[112,512]{1,0:T(8,128)S(1)}, f32[112,512]{1,0:T(8,128)}, u32[]{:S(2)}) copy-start(f32[112,512]{1,0:T(8,128)} %get-tuple-element.35) | copy-start | bytes 688132

commit v3 on v2

--- a/solution.py
+++ b/solution.py
@@ -373,12 +373,29 @@
         token_at = pl.ds(pl.multiple_of(c * CH, CH), CH)
         key_at = pl.ds(pl.multiple_of(c * keys, keys), keys)
         heads = [slice(h * DH, (h + 1) * DH) for h in range(cols // DH)]
-        q_rows, g_rows = q[token_at, :], g[token_at, :]
-        k_rows, v_rows = both[:, :cols], both[:, cols:]
+        blank = jnp.zeros((CH, DH), jnp.bfloat16)
+        corners = [
+            jnp.concatenate(
+                [
+                    jnp.concatenate([q[token_at, at], blank], axis=1),
+                    jnp.concatenate([blank, g[token_at, at]], axis=1),
+                ],
+                axis=0,
+            )
+            for at in heads
+        ]
         scale = 1.0 / math.sqrt(DH)
-        scores = jnp.concatenate([dot(q_rows[:, at], k_rows[:, at], 1, 1) for at in heads], axis=0)
-        dprobs = jnp.concatenate([dot(g_rows[:, at], v_rows[:, at], 1, 1) for at in heads], axis=0)
-        scores = scores * scale
+        products = [
+            dot(
+                corner,
+                jnp.concatenate([both[:, at], both[:, cols + at.start : cols + at.stop]], axis=1),
+                1,
+                1,
+            )
+            for corner, at in zip(corners, heads)
+        ]
+        scores = jnp.concatenate([product[:CH] for product in products], axis=0) * scale
+        dprobs = jnp.concatenate([product[CH:] for product in products], axis=0)
         shifted = jnp.exp(scores - jnp.max(scores, axis=-1, keepdims=True))
         probs = shifted * (1.0 / jnp.sum(shifted, axis=-1, keepdims=True))
         delta = jnp.sum(probs * dprobs, axis=-1, keepdims=True)
@@ -386,11 +403,11 @@
         half = probs.astype(jnp.bfloat16)
         for h, at in enumerate(heads):
             rows = slice(h * CH, (h + 1) * CH)
-            grads[key_at, at] = dot(dscores[rows], q_rows[:, at], 0, 0).astype(jnp.bfloat16)
-            grads[key_at, cols + at.start : cols + at.stop] = dot(
-                half[rows], g_rows[:, at], 0, 0
-            ).astype(jnp.bfloat16)
-            dq[token_at, at] = dot(dscores[rows], k_rows[:, at], 1, 0).astype(jnp.bfloat16)
+            pair_rows = jnp.concatenate([dscores[rows], half[rows]], axis=0)
+            grad = dot(pair_rows, corners[h], 0, 0).astype(jnp.bfloat16)
+            grads[key_at, at] = grad[:, :DH]
+            grads[key_at, cols + at.start : cols + at.stop] = grad[:, DH:]
+            dq[token_at, at] = dot(dscores[rows], both[:, at], 1, 0).astype(jnp.bfloat16)
 
     def near_copy(out, landed, sems, i):
         return remote(out.at[i], landed.at[i], sems.at[0, i], sems.at[1, i], near)
@@ -507,17 +524,9 @@
 
     group(0)
     loop(1, s_groups, group_step)
-    loop(0, w_groups, weight_send)
+    weight_send(0)
     slot_pairs(s_groups - 1)
-    query_terms(0)
-
-    def query_step(i):
-        query_terms(i)
-        query_pairs(i - 1)
-
-    loop(1, q_groups, query_step)
-    loop(0, w_groups, weight_keep)
-    query_pairs(q_groups - 1)
+    loop(1, w_groups, weight_send)
     loop(0, s_groups, slot_sums)
     for k in range(1, n):
         there = lax.rem(me + k, n)
@@ -526,7 +535,14 @@
         back_copy(k).start()
     for r in range(cap):
         ret_ref[me, r] = s_sum[slot_ref[me * cap + r]]
-    loop(0, w_groups, weight_pairs)
+
+    def late_step(i):
+        query_terms(i)
+        weight_keep(i)
+        weight_pairs(i)
+        query_pairs(i)
+
+    loop(0, q_groups, late_step)
     loop(0, q_groups, query_sums)
     for i in range(w_groups):
         total = weight_sums(i)
@@ -560,7 +576,15 @@
     gather_sent()
 
 
-def scatter_kernel(index_ref, ret_ref, out_ref, total):
+def scatter_kernel(
+    index_ref, ret_ref, qi_in, kw_in, vw_in, out_ref, qi_out, kw_out, vw_out, total, sems
+):
+    copies = [
+        pltpu.make_async_copy(src, dst, sems.at[i])
+        for i, (src, dst) in enumerate([(qi_in, qi_out), (kw_in, kw_out), (vw_in, vw_out)])
+    ]
+    for copy in copies:
+        copy.start()
     total[...] = jnp.zeros_like(total)
     senders, cap = ret_ref.shape[:2]
 
@@ -581,6 +605,8 @@
         return carry
 
     lax.fori_loop(0, total.shape[0], turn, 0)
+    for copy in copies:
+        copy.wait()
 
 
 def call(kernel, out_shape, scratch, collective=None, **kwargs):
@@ -722,13 +748,18 @@
         key_weight,
         value_weight,
     )
-    encodings_grad = call(
+    encodings_grad, query_input_grad, key_grad, value_grad = call(
         scatter_kernel,
-        sds((own_blocks, quarter, NTOK), bf16),
-        [pltpu.VMEM((own_blocks, quarter, NTOK), f32)],
-        in_specs=[pl.BlockSpec(memory_space=pltpu.SMEM), vmem],
-        out_specs=vmem,
-    )(asked.reshape(-1), returned)
+        [
+            sds((own_blocks, quarter, NTOK), bf16),
+            sds(query_input_grad.shape, bf16),
+            sds(key_grad.shape, f32),
+            sds(value_grad.shape, f32),
+        ],
+        [pltpu.VMEM((own_blocks, quarter, NTOK), f32), dma((3,))],
+        in_specs=[pl.BlockSpec(memory_space=pltpu.SMEM), vmem] + [anywhere] * 3,
+        out_specs=[vmem] + [anywhere] * 3,
+    )(asked.reshape(-1), returned, query_input_grad, key_grad, value_grad)
     return query_input_grad, jnp.swapaxes(encodings_grad, 1, 2), key_grad, value_grad
 
 

time: 135 us -> 177 us (1.31)
  Pallas kernels: 121 us -> 167 us
  local copies, waits for them, and re-layouts: 10.6 us -> 7.11 us
    pallas_call x1, Pallas kernels: 2.85 us -> 48.9 us  [shards(): call(scatter_kernel, [sds((own_blocks, quarter, NTOK), bf16), sds(query_i...]
    unnamed x13 -> x8, local copies, waits for them, and re-layouts: 5.45 us -> 1.94 us
where the time goes in v3:
time: 177 us
  Pallas kernels  167 us (94%)
  local copies, waits for them, and re-layouts  7.11 us (4%)
    pallas_call x1, Pallas kernels, shards(): call(functools.partial(exchange_kernel, n, cap), [sds((q_rows, q_width),...  109 us
    pallas_call x1, Pallas kernels, shards(): call(scatter_kernel, [sds((own_blocks, quarter, NTOK), bf16), sds(query_i...  48.9 us
    pallas_call x1, Pallas kernels, shards(): call(functools.partial(places_kernel, n), sds((n, 8, 128), i32), [pltpu.V...  9.73 us

profile of v3, /device:TPU:0, one launch (start us, length us, event | category | flops | bytes accessed | tf_op | source)
XLA Modules:
  0.0 176.8 jit_solution(2958903479403230279)
XLA Ops:
  0.6 0.0 copy-start
  0.6 1.2 copy-done
  1.8 0.8 copy.14
  2.6 0.1 reshape.199
  2.7 1.3 gather_fusion
  4.0 0.0 copy-start.1
  4.0 0.2 convert_reduce_fusion.1.rank_ref
  4.2 0.0 copy-start.2
  4.2 0.1 select_reduce_fusion
  4.4 0.1 copy.16
  4.5 0.7 reshape.201.slot_ref
  5.1 0.6 scatter.4.mine_ref
  5.7 9.7 %shard_map.111 = s32[8,8,128]{2,1,0:T(8,128)} custom-call(s32[8,128]{1,0:T(8,128)} %scatter.4.mine_ref), custom_call_target="tpu_custom_call" | custom-call | tf_op jit(solution)/shard_map/pallas_call | solution.py:651
  15.5 0.8 fusion.2
  16.3 0.2 convert_reduce_fusion
  16.5 0.1 select_reduce_fusion.1
  16.7 0.1 copy.17
  16.8 0.1 reshape.212
  16.8 0.1 copy.15
  16.9 0.6 sub.17.index_ref
  17.5 1.6 gather_fusion.1
  19.1 0.0 copy-done.1
  19.1 0.0 copy-done.2
  19.1 108.8 %shard_map.112 = (bf16[512,1024]{1,0:T(8,128)(2,1)}, bf16[8,2,224,128]{3,2,1,0:T(8,128)(2,1)}, f32[112,512]{1,0:T(8,128)}, f32[112,512]{1,0:T(8,128)}) custom-call(s32[16]{0:T(128)} %copy-done.1, s32[16]{0:T(128)} %copy-done.2, s32[16]{0:T(128)} %reshape.201.slot_ref, bf16[8,2,224,128]{3,2,1,0:T(8,128)(2,1)} %bitcast.11, bf16[512,512]{1,0:T(8,128)(2,1)} %q_hbm.1, ...), custom_call_target="tpu_custom_call" | custom-call | tf_op jit(solution)/shard_map/pallas_call | solution.py:728
  127.9 48.9 %shard_map.113 = (bf16[16,224,128]{2,1,0:T(8,128)(2,1)}, bf16[512,1024]{1,0:T(8,128)(2,1)}, f32[112,512]{1,0:T(8,128)}, f32[112,512]{1,0:T(8,128)}) custom-call(s32[16]{0:T(128)} %sub.17.index_ref, bf16[8,2,224,128]{3,2,1,0:T(8,128)(2,1)} %get-tuple-element.24.ret_ref, bf16[512,1024]{1,0:T(8,128)(2,1)} %get-tuple-element.25.qi_in, ...), custom_call_target="tpu_custom_call" | custom-call | tf_op jit(solution)/shard_map/pallas_call | solution.py:751
  (10 shorter events, 0.1 us)
Async XLA Ops:
  0.6 1.2 copy-start
  4.0 15.1 %copy-start.1 = (s32[16]{0:T(128)}, s32[16]{0:T(128)S(1)}, u32[]{:S(2)}) copy-start(s32[16]{0:T(128)S(1)} %and_select_fusion.2.dev_ref) | copy-start | bytes 196
  4.2 14.9 %copy-start.2 = (s32[16]{0:T(128)}, s32[16]{0:T(128)S(1)}, u32[]{:S(2)}) copy-start(s32[16]{0:T(128)S(1)} %convert_reduce_fusion.1.rank_ref) | copy-start | bytes 196

commit v4 on v3

--- a/solution.py
+++ b/solution.py
@@ -259,7 +259,7 @@
     dev_ref,
     rank_ref,
     slot_ref,
-    packed_hbm,
+    packed_ref,
     q_hbm,
     g_hbm,
     qw_hbm,
@@ -358,7 +358,7 @@
             load.wait()
 
     gather_sent = gather_steps(
-        n, packed_hbm, got, local_sem, ga_sem, gy_sem, gs_sem, gf_sem, weights_ready, project
+        n, packed_ref, got, local_sem, ga_sem, gy_sem, gs_sem, gf_sem, weights_ready, project
     )
     for load in loads[2:]:
         load.wait()
@@ -526,7 +526,15 @@
     loop(1, s_groups, group_step)
     weight_send(0)
     slot_pairs(s_groups - 1)
-    loop(1, w_groups, weight_send)
+    early = q_groups // 2
+
+    def early_step(i):
+        query_terms(i)
+        weight_send(i + 1)
+        query_pairs(i)
+
+    loop(0, early, early_step)
+    loop(early + 1, w_groups, weight_send)
     loop(0, s_groups, slot_sums)
     for k in range(1, n):
         there = lax.rem(me + k, n)
@@ -537,12 +545,18 @@
         ret_ref[me, r] = s_sum[slot_ref[me * cap + r]]
 
     def late_step(i):
-        query_terms(i)
+        query_terms(early + i)
         weight_keep(i)
         weight_pairs(i)
-        query_pairs(i)
-
-    loop(0, q_groups, late_step)
+        query_pairs(early + i)
+
+    loop(0, q_groups - early, late_step)
+
+    def last_step(i):
+        weight_keep(i)
+        weight_pairs(i)
+
+    loop(q_groups - early, w_groups, last_step)
     loop(0, q_groups, query_sums)
     for i in range(w_groups):
         total = weight_sums(i)
@@ -577,14 +591,11 @@
 
 
 def scatter_kernel(
-    index_ref, ret_ref, qi_in, kw_in, vw_in, out_ref, qi_out, kw_out, vw_out, total, sems
+    index_ref, ret_ref, qi_in, kw_in, vw_in, out_ref, qi_out, kw_out, vw_out, total
 ):
-    copies = [
-        pltpu.make_async_copy(src, dst, sems.at[i])
-        for i, (src, dst) in enumerate([(qi_in, qi_out), (kw_in, kw_out), (vw_in, vw_out)])
-    ]
-    for copy in copies:
-        copy.start()
+    qi_out[...] = qi_in[...]
+    kw_out[...] = kw_in[...]
+    vw_out[...] = vw_in[...]
     total[...] = jnp.zeros_like(total)
     senders, cap = ret_ref.shape[:2]
 
@@ -605,8 +616,6 @@
         return carry
 
     lax.fori_loop(0, total.shape[0], turn, 0)
-    for copy in copies:
-        copy.wait()
 
 
 def call(kernel, out_shape, scratch, collective=None, **kwargs):
@@ -735,7 +744,7 @@
         ],
         scratch,
         collective=1,
-        in_specs=[pl.BlockSpec(memory_space=pltpu.SMEM)] * 3 + [anywhere] * 6,
+        in_specs=[pl.BlockSpec(memory_space=pltpu.SMEM)] * 3 + [vmem] + [anywhere] * 5,
         out_specs=[vmem] * 4,
     )(
         owner,
@@ -756,9 +765,9 @@
             sds(key_grad.shape, f32),
             sds(value_grad.shape, f32),
         ],
-        [pltpu.VMEM((own_blocks, quarter, NTOK), f32), dma((3,))],
-        in_specs=[pl.BlockSpec(memory_space=pltpu.SMEM), vmem] + [anywhere] * 3,
-        out_specs=[vmem] + [anywhere] * 3,
+        [pltpu.VMEM((own_blocks, quarter, NTOK), f32)],
+        in_specs=[pl.BlockSpec(memory_space=pltpu.SMEM), vmem, vmem, vmem, vmem],
+        out_specs=[vmem] * 4,
     )(asked.reshape(-1), returned, query_input_grad, key_grad, value_grad)
     return query_input_grad, jnp.swapaxes(encodings_grad, 1, 2), key_grad, value_grad
 

time: 177 us -> 132 us (0.75)
  Pallas kernels: 167 us -> 123 us
    pallas_call x1, Pallas kernels: 48.9 us -> 3.86 us  [shards(): call(scatter_kernel, [sds((own_blocks, quarter, NTOK), bf16), sds(query_i...]
where the time goes in v4:
time: 132 us
  Pallas kernels  123 us (93%)
  local copies, waits for them, and re-layouts  7.11 us (5%)
  other arithmetic  1.55 us (1%)
    pallas_call x1, Pallas kernels, shards(): call(functools.partial(exchange_kernel, n, cap), [sds((q_rows, q_width),...  109 us
    pallas_call x1, Pallas kernels, shards(): call(functools.partial(places_kernel, n), sds((n, 8, 128), i32), [pltpu.V...  9.73 us
    pallas_call x1, Pallas kernels, shards(): call(scatter_kernel, [sds((own_blocks, quarter, NTOK), bf16), sds(query_i...  3.86 us

profile of v4, /device:TPU:0, one launch (start us, length us, event | category | flops | bytes accessed | tf_op | source)
XLA Modules:
  0.0 131.9 jit_solution(13440400535060536842)
XLA Ops:
  0.6 0.0 copy-start
  0.6 1.2 copy-done
  1.8 0.8 copy.14
  2.6 0.1 reshape.199
  2.7 1.3 gather_fusion
  4.0 0.0 copy-start.1
  4.0 0.2 convert_reduce_fusion.1.rank_ref
  4.2 0.0 copy-start.2
  4.2 0.1 select_reduce_fusion
  4.4 0.1 copy.16
  4.5 0.7 reshape.201.slot_ref
  5.1 0.6 scatter.4.mine_ref
  5.7 9.7 %shard_map.111 = s32[8,8,128]{2,1,0:T(8,128)} custom-call(s32[8,128]{1,0:T(8,128)} %scatter.4.mine_ref), custom_call_target="tpu_custom_call" | custom-call | tf_op jit(solution)/shard_map/pallas_call | solution.py:660
  15.5 0.8 fusion.2
  16.3 0.2 convert_reduce_fusion
  16.5 0.1 select_reduce_fusion.1
  16.7 0.1 copy.17
  16.8 0.1 reshape.212
  16.8 0.1 copy.15
  16.9 0.6 sub.17.index_ref
  17.5 1.6 %gather_fusion.1 = bf16[16,224,128]{2,1,0:T(8,128)(2,1)} fusion(bf16[16,224,128]{2,1,0:T(8,128)(2,1)S(1)} %bitcast.10, s32[1024]{0:T(1024)S(1)} %pad_clamp_fusion), kind=kCustom, calls=%fused_computation.1 | custom fusion | bytes 1835072 | tf_op jit(solution)/shard_map/gather | solution.py:682
  19.1 0.0 copy-done.1
  19.1 0.0 copy-done.2
  19.1 108.9 %shard_map.112 = (bf16[512,1024]{1,0:T(8,128)(2,1)}, bf16[8,2,224,128]{3,2,1,0:T(8,128)(2,1)}, f32[112,512]{1,0:T(8,128)}, f32[112,512]{1,0:T(8,128)}) custom-call(s32[16]{0:T(128)} %copy-done.1, s32[16]{0:T(128)} %copy-done.2, s32[16]{0:T(128)} %reshape.201.slot_ref, bf16[8,2,224,128]{3,2,1,0:T(8,128)(2,1)} %bitcast.11, bf16[512,512]{1,0:T(8,128)(2,1)} %q_hbm.1, ...), custom_call_target="tpu_custom_call" | custom-call | tf_op jit(solution)/shard_map/pallas_call | solution.py:737
  128.1 3.9 %shard_map.113 = (bf16[16,224,128]{2,1,0:T(8,128)(2,1)}, bf16[512,1024]{1,0:T(8,128)(2,1)}, f32[112,512]{1,0:T(8,128)}, f32[112,512]{1,0:T(8,128)}) custom-call(s32[16]{0:T(128)} %sub.17.index_ref, bf16[8,2,224,128]{3,2,1,0:T(8,128)(2,1)} %get-tuple-element.24.ret_ref, bf16[512,1024]{1,0:T(8,128)(2,1)} %get-tuple-element.25.qi_in, ...), custom_call_target="tpu_custom_call" | custom-call | tf_op jit(solution)/shard_map/pallas_call | solution.py:760
  (10 shorter events, 0.1 us)
Async XLA Ops:
  0.6 1.2 copy-start
  4.0 15.1 %copy-start.1 = (s32[16]{0:T(128)}, s32[16]{0:T(128)S(1)}, u32[]{:S(2)}) copy-start(s32[16]{0:T(128)S(1)} %and_select_fusion.2.dev_ref) | copy-start | bytes 196
  4.2 14.9 %copy-start.2 = (s32[16]{0:T(128)}, s32[16]{0:T(128)S(1)}, u32[]{:S(2)}) copy-start(s32[16]{0:T(128)S(1)} %convert_reduce_fusion.1.rank_ref) | copy-start | bytes 196

commit v5 on v4

--- a/solution.py
+++ b/solution.py
@@ -277,16 +277,14 @@
     q,
     g,
     qw,
-    wk,
-    wv,
+    wkv,
     load_sem,
     local_sem,
     ga_sem,
     gy_sem,
     gs_sem,
     gf_sem,
-    s_own,
-    s_out,
+    s_terms,
     s_in,
     s_far,
     s_far_in,
@@ -319,12 +317,13 @@
     side, line = lax.rem(me, 2), me // 2
     lines = n // 2
     pair = {"dp": me + 1 - 2 * side}
+    cols = wk_hbm.shape[1]
     loads = [
         pltpu.make_async_copy(src, dst, load_sem.at[i])
         for i, (src, dst) in enumerate(
             [
-                (wk_hbm, wk),
-                (wv_hbm, wv),
+                (wk_hbm, wkv.at[:, pl.ds(0, cols)]),
+                (wv_hbm, wkv.at[:, pl.ds(cols, cols)]),
                 (q_hbm, q),
                 (g_hbm, g),
                 (qw_hbm, qw),
@@ -335,7 +334,6 @@
         load.start()
     greet([{"dp": lax.rem(me + k, n)} for k in range(1, n)] + [far, near])
     s_groups, quarter, s_cols = s_far.shape
-    cols = wk.shape[1]
     q_groups, q_rows, q_cols = q_far.shape
     w_groups, w_rows, w_cols = w_own.shape[0], w_own.shape[2], w_own.shape[3]
 
@@ -344,14 +342,9 @@
 
     def project(sender):
         rows = jnp.concatenate(
-            [got[sender, :, r].reshape(wk.shape[0], NTOK) for r in range(cap)], axis=1
-        )
-        kv[sender, :, :, :cols] = (
-            dot(rows, wk[...], 0, 0).astype(jnp.bfloat16).reshape(cap, NTOK, cols)
-        )
-        kv[sender, :, :, cols:] = (
-            dot(rows, wv[...], 0, 0).astype(jnp.bfloat16).reshape(cap, NTOK, cols)
-        )
+            [got[sender, :, r].reshape(wkv.shape[0], NTOK) for r in range(cap)], axis=1
+        )
+        kv[sender] = dot(rows, wkv[...], 0, 0).astype(jnp.bfloat16).reshape(cap, NTOK, 2 * cols)
 
     def weights_ready():
         for load in loads[:2]:
@@ -417,22 +410,24 @@
 
     def slot_terms(i):
         at = pl.ds(pl.multiple_of(i * s_cols, s_cols), s_cols)
-        key_rows, value_rows = grads[at, :cols], grads[at, cols:]
-        for part in range(2):
-            for target, owner in ((s_out, 1 - low), (s_own, low)):
-                rows = pl.ds(pl.multiple_of((2 * part + owner) * quarter, 16), quarter)
-                term = dot(wk[rows, :], key_rows, 1, 1) + dot(wv[rows, :], value_rows, 1, 1)
-                target[i, part] = term.astype(jnp.bfloat16)
-        near_copy(s_out, s_in, ss_sem, i).start()
+        terms = dot(wkv[...], grads[at, :], 1, 1).astype(jnp.bfloat16)
+        for owner in range(4):
+            s_terms[i, owner % 2, owner // 2] = terms[owner * quarter : (owner + 1) * quarter]
+        slot_copy(i).start()
+
+    def slot_copy(i):
+        return remote(
+            s_terms.at[i, 1 - low], s_in.at[i], ss_sem.at[0, i], ss_sem.at[1, i], near
+        )
 
     def slot_pairs(i):
-        near_copy(s_out, s_in, ss_sem, i).wait_recv()
-        s_far[i] = (f32(s_own[i, 1 - high]) + f32(s_in[i, 1 - high])).astype(jnp.bfloat16)
+        slot_copy(i).wait_recv()
+        s_far[i] = (f32(s_terms[i, low, 1 - high]) + f32(s_in[i, 1 - high])).astype(jnp.bfloat16)
         far_copy(s_far, s_far_in, sy_sem, i).start()
 
     def slot_sums(i):
         far_copy(s_far, s_far_in, sy_sem, i).wait_recv()
-        total = (f32(s_own[i, high]) + f32(s_in[i, high]) + f32(s_far_in[i])).astype(jnp.bfloat16)
+        total = (f32(s_terms[i, low, high]) + f32(s_in[i, high]) + f32(s_far_in[i])).astype(jnp.bfloat16)
         per = s_cols // NTOK
         for j in range(per):
             s_sum[i * per + j] = total[:, j * NTOK : (j + 1) * NTOK]
@@ -457,20 +452,21 @@
             jnp.bfloat16
         )
 
-    def weight_dot(i, which):
-        at = pl.ds(pl.multiple_of(i * w_cols, w_cols), w_cols)
-        rows = blocks[:, which].reshape(lines * w_rows, blocks.shape[3])
-        return dot(rows, grads[:, at], 1, 0).reshape(lines, w_rows, w_cols)
-
     def weight_copy(i):
         return remote(w_out.at[i], w_in.at[i], wx_sem.at[0, i], wx_sem.at[1, i], pair)
 
     def weight_send(i):
-        w_out[i] = weight_dot(i, 1 - side).astype(jnp.bfloat16)
+        at = pl.ds(pl.multiple_of(i * w_cols, w_cols), w_cols)
+        rows = blocks[...].reshape(2 * lines * w_rows, blocks.shape[3])
+        terms = dot(rows, grads[:, at], 1, 0).reshape(lines, 2, w_rows, w_cols)
+        for which in range(2):
+
+            @pl.when(side == which)
+            def _():
+                w_out[i] = terms[:, 1 - which].astype(jnp.bfloat16)
+                w_own[i] = terms[:, which]
+
         weight_copy(i).start()
-
-    def weight_keep(i):
-        w_own[i] = weight_dot(i, side)
 
     def line_copy(i, k, sign):
         there = 2 * lax.rem(line + sign * k + lines, lines) + side
@@ -546,14 +542,12 @@
 
     def late_step(i):
         query_terms(early + i)
-        weight_keep(i)
         weight_pairs(i)
         query_pairs(early + i)
 
     loop(0, q_groups - early, late_step)
 
     def last_step(i):
-        weight_keep(i)
         weight_pairs(i)
 
     loop(q_groups - early, w_groups, last_step)
@@ -568,7 +562,7 @@
         ret_ref[lax.rem(me - k + n, n)] = s_back_in[k - 1]
 
     def sent(i):
-        near_copy(s_out, s_in, ss_sem, i).wait_send()
+        slot_copy(i).wait_send()
         far_copy(s_far, s_far_in, sy_sem, i).wait_send()
 
     loop(0, s_groups, sent)
@@ -700,16 +694,14 @@
         buffer(q_rows, cols),
         buffer(q_rows, cols),
         buffer(*query_weight.shape),
-        buffer(depth, cols),
-        buffer(depth, cols),
+        buffer(depth, 2 * cols),
         dma((5,)),
         dma,
         dma((2, n)),
         dma((2, n)),
         dma((2, n)),
         dma((2, n)),
-        buffer(groups, 2, quarter, s_cols),
-        buffer(groups, 2, quarter, s_cols),
+        buffer(groups, 2, 2, quarter, s_cols),
         buffer(groups, 2, quarter, s_cols),
         buffer(groups, quarter, s_cols),
         buffer(groups, quarter, s_cols),

time: 132 us -> 132 us (level)
  no operation moved by 1% of the time
where the time goes in v5:
time: 132 us; the launch traced here: 131 us
  Pallas kernels  122 us (92%)
  local copies, waits for them, and re-layouts  7.11 us (5%)
  other arithmetic  1.55 us (1%)
    pallas_call x1, Pallas kernels, shards(): call(functools.partial(exchange_kernel, n, cap), [sds((q_rows, q_width),...  108 us
    pallas_call x1, Pallas kernels, shards(): call(functools.partial(places_kernel, n), sds((n, 8, 128), i32), [pltpu.V...  9.73 us
    pallas_call x1, Pallas kernels, shards(): call(scatter_kernel, [sds((own_blocks, quarter, NTOK), bf16), sds(query_i...  3.86 us

profile of v5, /device:TPU:0, one launch (start us, length us, event | category | flops | bytes accessed | tf_op | source)
XLA Modules:
  0.0 131.5 jit_solution(1150098986840041917)
XLA Ops:
  0.6 0.0 copy-start
  0.6 1.2 copy-done
  1.8 0.8 copy.14
  2.6 0.1 reshape.199
  2.7 1.3 %gather_fusion = s32[16]{0:T(128)S(1)} fusion(s32[128]{0:T(128)} %param.13, s32[1024]{0:T(1024)S(1)} %pad_clamp_fusion.1), kind=kCustom, calls=%fused_computation | custom fusion | bytes 192 | tf_op jit(solution)/shard_map/gather | solution.py:652
  4.0 0.0 copy-start.1
  4.0 0.2 convert_reduce_fusion.1.rank_ref
  4.2 0.0 copy-start.2
  4.2 0.1 select_reduce_fusion
  4.4 0.1 copy.16
  4.5 0.7 reshape.201.slot_ref
  5.1 0.6 scatter.4.mine_ref
  5.7 9.7 %shard_map.111 = s32[8,8,128]{2,1,0:T(8,128)} custom-call(s32[8,128]{1,0:T(8,128)} %scatter.4.mine_ref), custom_call_target="tpu_custom_call" | custom-call | tf_op jit(solution)/shard_map/pallas_call | solution.py:654
  15.5 0.8 fusion.2
  16.3 0.2 convert_reduce_fusion
  16.5 0.1 select_reduce_fusion.1
  16.7 0.1 copy.17
  16.8 0.1 reshape.212
  16.8 0.1 copy.15
  16.9 0.6 sub.17.index_ref
  17.5 1.6 %gather_fusion.1 = bf16[16,224,128]{2,1,0:T(8,128)(2,1)} fusion(bf16[16,224,128]{2,1,0:T(8,128)(2,1)S(1)} %bitcast.10, s32[1024]{0:T(1024)S(1)} %pad_clamp_fusion), kind=kCustom, calls=%fused_computation.1 | custom fusion | bytes 1835072 | tf_op jit(solution)/shard_map/gather | solution.py:676
  19.1 0.0 copy-done.1
  19.1 0.0 copy-done.2
  19.1 108.5 %shard_map.112 = (bf16[512,1024]{1,0:T(8,128)(2,1)}, bf16[8,2,224,128]{3,2,1,0:T(8,128)(2,1)}, f32[112,512]{1,0:T(8,128)}, f32[112,512]{1,0:T(8,128)}) custom-call(s32[16]{0:T(128)} %copy-done.1, s32[16]{0:T(128)} %copy-done.2, s32[16]{0:T(128)} %reshape.201.slot_ref, bf16[8,2,224,128]{3,2,1,0:T(8,128)(2,1)} %bitcast.11, bf16[512,512]{1,0:T(8,128)(2,1)} %q_hbm.1, ...), custom_call_target="tpu_custom_call" | custom-call | tf_op jit(solution)/shard_map/pallas_call | solution.py:729
  127.6 3.9 %shard_map.113 = (bf16[16,224,128]{2,1,0:T(8,128)(2,1)}, bf16[512,1024]{1,0:T(8,128)(2,1)}, f32[112,512]{1,0:T(8,128)}, f32[112,512]{1,0:T(8,128)}) custom-call(s32[16]{0:T(128)} %sub.17.index_ref, bf16[8,2,224,128]{3,2,1,0:T(8,128)(2,1)} %get-tuple-element.24.ret_ref, bf16[512,1024]{1,0:T(8,128)(2,1)} %get-tuple-element.25.qi_in, ...), custom_call_target="tpu_custom_call" | custom-call | tf_op jit(solution)/shard_map/pallas_call | solution.py:752
  (10 shorter events, 0.1 us)
Async XLA Ops:
  0.6 1.2 copy-start
  4.0 15.1 %copy-start.1 = (s32[16]{0:T(128)}, s32[16]{0:T(128)S(1)}, u32[]{:S(2)}) copy-start(s32[16]{0:T(128)S(1)} %and_select_fusion.2.dev_ref) | copy-start | bytes 196
  4.2 14.9 %copy-start.2 = (s32[16]{0:T(128)}, s32[16]{0:T(128)S(1)}, u32[]{:S(2)}) copy-start(s32[16]{0:T(128)S(1)} %convert_reduce_fusion.1.rank_ref) | copy-start | bytes 196
